TPU v7x, 32 devices: a whole 2x2x4 slice. The times are simulated.
32 devices in a mesh: groups: 2 (over y), expert: 4 (over x, core), dp: 4 (over z).
Axes of the slice: x: 2, y: 2, z: 4, core: 2. Of those that a mesh axis runs over, the one named last changes fastest.
Arguments:
- hidden_in: bfloat16 [4096, 1024], P(('groups', 'expert', 'dp')), parts along dimension 0, may hold values from -125 to 125
- context: bfloat16 [4096, 1024], P(('groups', 'expert', 'dp')), parts along dimension 0, may hold values from -6 to 6
- norm_gain: float32 [1024], replicated, may hold values from 0.1 to 1.9
- route_ids: int32 [4096, 8], P(('groups', 'expert', 'dp')), parts along dimension 0, may hold values from 0 to 31, all different within a row; in each aligned block of 128 rows (0 to 127, 128 to 255, ...) at most 36 rows name the same one
- route_weights: float32 [4096, 8], P(('groups', 'expert', 'dp')), parts along dimension 0, may hold values from 0.03 to 0.4
- w_gate: bfloat16 [32, 1024, 512], P('expert'), may hold values from -0.1875 to 0.1875
- w_up: bfloat16 [32, 1024, 512], P('expert'), may hold values from -0.1875 to 0.1875
- w_down: bfloat16 [32, 512, 1024], P('expert'), may hold values from -0.25 to 0.25
- out_grad: bfloat16 [4096, 1024], P(('groups', 'expert', 'dp')), parts along dimension 0, may hold values from -6 to 6
Outputs:
- moe_out: bfloat16 [4096, 1024], P(('groups', 'expert', 'dp')), parts along dimension 0
- branch_grad: bfloat16 [4096, 1024], P(('groups', 'expert', 'dp')), parts along dimension 0
- route_grad: float32 [4096, 8], P(('groups', 'expert', 'dp')), parts along dimension 0
- gain_grad: float32 [2048], P(('groups', 'expert', 'dp')), parts along dimension 0
- proj_grad: float32 [2048, 1024], P(('groups', 'expert', 'dp')), parts along dimension 0
- gate_grad: float32 [64, 1024, 512], P(('groups', 'expert'), 'dp'), parts along dimension 0
- up_grad: float32 [64, 1024, 512], P(('groups', 'expert'), 'dp'), parts along dimension 0
- down_grad: float32 [64, 512, 1024], P(('groups', 'expert'), 'dp'), parts along dimension 0
There are 2 independent parts, one for each index of `groups`. A program takes and returns all parts, laid end to end along the dimension named above; an argument that names none is the same for every part. Nothing has to cross between parts.
Inputs may be any that keep to these rules, and one draw needn't show every extreme that they name: `route_ids`: each row names 8 different experts; in each aligned block of 128 rows no expert is named by more than 36 rows, a bound that some block reaches.
All inputs are finite; a program needn't handle non-finite values.
Results may differ from a plain program's by a relative error of at most 0.0085.
Values may be sent and summed in bfloat16 or wider, within the bound.
A program may use at most 192 MiB of HBM per device.

v0:
```python
import math

import jax
import jax.numpy as jnp
from jax import lax
from jax.sharding import PartitionSpec as P

EPSILON = 1e-05


def silu_slope(pre_act):
    sigmoid_val = jax.nn.sigmoid(pre_act)
    return sigmoid_val * (1.0 + pre_act * (1.0 - sigmoid_val))


def forward_rows(rows_in, w_gate, w_up, w_down):
    gate_pre = jnp.einsum("sjcd,jdf->sjcf", rows_in, w_gate, preferred_element_type=jnp.float32)
    up_pre = jnp.einsum("sjcd,jdf->sjcf", rows_in, w_up, preferred_element_type=jnp.float32)
    hidden_act = (jax.nn.silu(gate_pre) * up_pre).astype(jnp.bfloat16)
    result = jnp.einsum(
        "sjcf,jfd->sjcd", hidden_act, w_down, preferred_element_type=jnp.float32
    ).astype(jnp.bfloat16)
    return (gate_pre, up_pre, hidden_act, result)


def backward_rows(
    rows_in, gate_pre, up_pre, hidden_act, rows_grad, w_gate, w_up, w_down, grad_scale
):
    inner_grad = jnp.einsum("sjcd,jfd->sjcf", rows_grad, w_down, preferred_element_type=jnp.float32)
    gate_delta = (inner_grad * up_pre * silu_slope(gate_pre)).astype(jnp.bfloat16)
    up_delta = (inner_grad * jax.nn.silu(gate_pre)).astype(jnp.bfloat16)
    input_delta = (
        jnp.einsum("sjcf,jdf->sjcd", gate_delta, w_gate, preferred_element_type=jnp.float32)
        + jnp.einsum("sjcf,jdf->sjcd", up_delta, w_up, preferred_element_type=jnp.float32)
    ).astype(jnp.bfloat16)
    gate_term = (
        jnp.einsum("sjcd,sjcf->jdf", rows_in, gate_delta, preferred_element_type=jnp.float32)
        * grad_scale
    )
    up_term = (
        jnp.einsum("sjcd,sjcf->jdf", rows_in, up_delta, preferred_element_type=jnp.float32)
        * grad_scale
    )
    down_term = (
        jnp.einsum("sjcf,sjcd->jfd", hidden_act, rows_grad, preferred_element_type=jnp.float32)
        * grad_scale
    )
    return (input_delta, gate_term, up_term, down_term)


def body(hidden_in, context, norm_gain, route_ids, route_weights, w_gate, w_up, w_down, out_grad):
    tok_rows = hidden_in.shape[0]
    feature_count = hidden_in.shape[1]
    top_count = route_ids.shape[1]
    local_experts = w_gate.shape[0]
    owners = lax.axis_size("expert")
    expert_total = local_experts * owners
    capacity = tok_rows * top_count * 9 // (8 * expert_total)
    token_total = tok_rows * owners * lax.axis_size("dp")
    grad_scale = 8.0 / math.sqrt(token_total)
    hidden = hidden_in.astype(jnp.float32)
    inv_rms = lax.rsqrt(jnp.mean(hidden * hidden, axis=-1, keepdims=True) + EPSILON)
    normed = hidden * inv_rms
    scaled_in = (normed * norm_gain).astype(jnp.bfloat16)
    flat_ids = route_ids.reshape(-1)
    one_hot = (flat_ids[:, None] == jnp.arange(expert_total, dtype=jnp.int32)[None, :]).astype(
        jnp.int32
    )
    earlier = jnp.cumsum(one_hot, axis=0) - one_hot
    position = jnp.sum(earlier * one_hot, axis=-1)
    target = flat_ids * capacity + position
    token_of = jnp.arange(tok_rows * top_count, dtype=jnp.int32) // top_count
    slot_token = jnp.zeros((expert_total * capacity,), jnp.int32).at[target].set(token_of)
    slot_live = jnp.zeros((expert_total * capacity,), jnp.int32).at[target].set(1)
    slot_weight = (
        jnp.zeros((expert_total * capacity,), jnp.float32).at[target].set(route_weights.reshape(-1))
    )
    live_mask = slot_live[:, None] > 0
    out_grad32 = out_grad.astype(jnp.float32)
    send_in = jnp.where(live_mask, scaled_in[slot_token], jnp.zeros((), jnp.bfloat16))
    send_grad = jnp.where(
        live_mask,
        (slot_weight[:, None] * out_grad32[slot_token]).astype(jnp.bfloat16),
        jnp.zeros((), jnp.bfloat16),
    )
    buffer_shape = (owners, local_experts, capacity, feature_count)
    send_in = send_in.reshape(buffer_shape)
    send_grad = send_grad.reshape(buffer_shape)
    got_in = lax.all_to_all(send_in, "expert", split_axis=0, concat_axis=0, tiled=True)
    gate_pre, up_pre, hidden_act, result = forward_rows(got_in, w_gate, w_up, w_down)
    back_out = lax.all_to_all(result, "expert", split_axis=0, concat_axis=0, tiled=True)
    got_grad = lax.all_to_all(send_grad, "expert", split_axis=0, concat_axis=0, tiled=True)
    input_delta, gate_term, up_term, down_term = backward_rows(
        got_in, gate_pre, up_pre, hidden_act, got_grad, w_gate, w_up, w_down, grad_scale
    )
    back_delta = lax.all_to_all(input_delta, "expert", split_axis=0, concat_axis=0, tiled=True)
    gate_grad, up_grad, down_grad = (
        lax.psum_scatter(
            gate_term.astype(jnp.bfloat16), "dp", scatter_dimension=1, tiled=True
        ).astype(jnp.float32),
        lax.psum_scatter(
            up_term.astype(jnp.bfloat16), "dp", scatter_dimension=1, tiled=True
        ).astype(jnp.float32),
        lax.psum_scatter(
            down_term.astype(jnp.bfloat16), "dp", scatter_dimension=1, tiled=True
        ).astype(jnp.float32),
    )
    take_out = back_out.reshape(expert_total * capacity, feature_count)[target].reshape(
        tok_rows, top_count, feature_count
    )
    take_delta = back_delta.reshape(expert_total * capacity, feature_count)[target].reshape(
        tok_rows, top_count, feature_count
    )
    moe_out = jnp.sum(route_weights[..., None] * take_out.astype(jnp.float32), axis=1).astype(
        jnp.bfloat16
    )
    route_grad = jnp.einsum("tkd,td->tk", take_out, out_grad, preferred_element_type=jnp.float32)
    norm_delta = jnp.sum(take_delta.astype(jnp.float32), axis=1)
    scaled_delta = norm_delta * norm_gain
    branch = inv_rms * (
        scaled_delta - normed * jnp.mean(scaled_delta * normed, axis=-1, keepdims=True)
    )
    branch_grad = branch.astype(jnp.bfloat16)
    full_grad = (out_grad32 + branch).astype(jnp.bfloat16)
    proj_term = lax.dot_general(
        context, full_grad, (((0,), (0,)), ((), ())), preferred_element_type=jnp.float32
    ) / math.sqrt(token_total)
    gain_term = jnp.sum(norm_delta * normed, axis=0) * grad_scale
    proj_grad, gain_grad = (
        lax.psum_scatter(proj_term, ("expert", "dp"), scatter_dimension=0, tiled=True),
        lax.psum_scatter(gain_term, ("expert", "dp"), scatter_dimension=0, tiled=True),
    )
    return (moe_out, branch_grad, route_grad, gain_grad, proj_grad, gate_grad, up_grad, down_grad)


def solution(mesh):
    return jax.shard_map(
        body,
        mesh=mesh,
        in_specs=(
            P(("groups", "expert", "dp"), None),
            P(("groups", "expert", "dp"), None),
            P(),
            P(("groups", "expert", "dp"), None),
            P(("groups", "expert", "dp"), None),
            P("expert", None, None),
            P("expert", None, None),
            P("expert", None, None),
            P(("groups", "expert", "dp"), None),
        ),
        out_specs=(
            P(("groups", "expert", "dp"), None),
            P(("groups", "expert", "dp"), None),
            P(("groups", "expert", "dp"), None),
            P(("groups", "expert", "dp")),
            P(("groups", "expert", "dp"), None),
            P(("groups", "expert"), "dp", None),
            P(("groups", "expert"), "dp", None),
            P(("groups", "expert"), "dp", None),
        ),
        check_vma=False,
    )
```

profile of v0, /device:TPU:0, one launch (start us, length us, event | category | flops | bytes accessed | tf_op | source)
XLA Modules:
  0.0 674.5 jit_solution(16252043731865860476)
XLA Ops:
  11.1 9.0 %reduce-window.6 = s32[32,8,128]{2,1,0:T(8,128)S(1)} reduce-window(s32[32,8,128]{2,1,0:T(8,128)S(1)} %fusion.53, s32[]{:T(128)} %constant.18.clone.1), window={size=1x1x128 pad=0_0x0_0x127_0}, to_apply=%region_0.0 | reduce-window | flops 4161536 | bytes 262148 | tf_op jit(solution)/shard_map/reduce-window
  35.1 5.0 gather_fusion
  42.6 5.0 gather_fusion.2
  47.6 5.2 gather.20
  68.1 24.1 %all-to-all-done = bf16[4,8,36,1024]{3,1,2,0:T(8,128)(2,1)S(1)} async-done(((bf16[4,8,36,1024]{3,1,2,0:T(8,128)(2,1)}), bf16[4,8,36,1024]{3,1,2,0:T(8,128)(2,1)S(1)}, u32[]{:S(2)}, u32[]{:S(2)}) %all-to-all-start) | async-done | bytes 2359328 | tf_op jit(solution)/shard_map/all_to_all | solution.py:89
  97.3 8.3 %fusion.5 = f32[8,4,36,512]{3,2,1,0:T(8,128)} fusion(bf16[8,1024,512]{2,1,0:T(8,128)(2,1)} %param.15, bf16[4,8,36,1024]{3,1,2,0:T(8,128)(2,1)S(1)} %all-to-all-done), kind=kOutput, calls=%fused_computation.15 | convolution fusion | flops 1207959552 | bytes 13107200 | tf_op jit(solution)/shard_map/sjcd,jdf->sjcf/dot_general | solution.py:18
  105.6 8.3 %fusion.9 = f32[8,4,36,512]{3,2,1,0:T(8,128)} fusion(bf16[8,1024,512]{2,1,0:T(8,128)(2,1)} %param.14, bf16[4,8,36,1024]{3,1,2,0:T(8,128)(2,1)S(1)} %all-to-all-done), kind=kOutput, calls=%fused_computation.19 | convolution fusion | flops 1207959552 | bytes 13107200 | tf_op jit(solution)/shard_map/sjcd,jdf->sjcf/dot_general | solution.py:17
  113.9 11.4 %all-to-all-done.2 = bf16[4,8,36,1024]{3,1,2,0:T(8,128)(2,1)} async-done(((bf16[4,8,36,1024]{3,1,2,0:T(8,128)(2,1)}), bf16[4,8,36,1024]{3,1,2,0:T(8,128)(2,1)}, u32[]{:S(2)}, u32[]{:S(2)}) %all-to-all-start.2) | async-done | bytes 2359328 | tf_op jit(solution)/shard_map/all_to_all | solution.py:92
  125.3 11.9 %fusion.18 = (bf16[4,8,36,512]{3,2,0,1:T(8,128)(2,1)}, bf16[4,8,36,512]{3,2,0,1:T(8,128)(2,1)S(1)}, bf16[4,8,36,512]{3,2,0,1:T(8,128)(2,1)}) fusion(f32[8,4,36,512]{3,2,1,0:T(8,128)} %fusion.5, f32[8,4,36,512]{3,2,1,0:T(8,128)} %fusion.9, bf16[8,512,1024]{2,1,0:T(8,128)(2,1)} %param.16, bf16[4,8,36,1024]{3,1,2,0:T(8,128)(2,1)} %all-to-all-done.2), kind=kOutput, calls=%fused_computation.35 | convolution fusion | flops 1216806912 | bytes 19005440 | tf_op jit(solution)/shard_map/sjcd,jfd->sjcf/dot_general | solution.py:29
  138.3 9.7 %fusion = bf16[8,512,1024]{2,1,0:T(8,128)(2,1)} fusion(bf16[4,8,36,512]{3,2,0,1:T(8,128)(2,1)S(1)} %get-tuple-element.35, bf16[4,8,36,1024]{3,1,2,0:T(8,128)(2,1)} %all-to-all-done.2), kind=kOutput, calls=%fused_computation.8 | convolution fusion | flops 1216348160 | bytes 11927552 | tf_op jit(solution)/shard_map/sjcf,sjcd->jfd/dot_general | solution.py:45
  148.1 10.0 %fusion.2 = bf16[8,1024,512]{2,1,0:T(8,128)(2,1)} fusion(bf16[4,8,36,512]{3,2,0,1:T(8,128)(2,1)} %get-tuple-element.34, bf16[4,8,36,1024]{3,1,2,0:T(8,128)(2,1)S(1)} %all-to-all-done), kind=kOutput, calls=%fused_computation.12 | convolution fusion | flops 1216348160 | bytes 11927552 | tf_op jit(solution)/shard_map/sjcd,sjcf->jdf/dot_general | solution.py:37
  158.4 9.8 %fusion.1 = bf16[8,1024,512]{2,1,0:T(8,128)(2,1)} fusion(bf16[4,8,36,512]{3,2,0,1:T(8,128)(2,1)} %get-tuple-element.36, bf16[4,8,36,1024]{3,1,2,0:T(8,128)(2,1)S(1)} %all-to-all-done), kind=kOutput, calls=%fused_computation.10 | convolution fusion | flops 1216348160 | bytes 11927552 | tf_op jit(solution)/shard_map/sjcd,sjcf->jdf/dot_general | solution.py:41
  169.5 6.4 fusion.3
  175.9 6.2 fusion.16
  188.8 28.2 %all-to-all-done.3 = bf16[4,8,36,1024]{3,1,2,0:T(8,128)(2,1)S(1)} async-done(((bf16[4,8,36,1024]{3,1,2,0:T(8,128)(2,1)}), bf16[4,8,36,1024]{3,1,2,0:T(8,128)(2,1)S(1)}, u32[]{:S(2)}, u32[]{:S(2)}) %all-to-all-start.3) | async-done | bytes 2359328 | tf_op jit(solution)/shard_map/all_to_all | solution.py:96
  222.6 5.3 gather_fusion.3
  234.1 5.3 copy.61
  240.8 5.0 convert_bitcast_fusion
  253.5 27.2 %all-to-all-done.1 = bf16[4,8,36,1024]{3,1,2,0:T(8,128)(2,1)S(1)} async-done(((bf16[4,8,36,1024]{3,1,2,0:T(8,128)(2,1)}), bf16[4,8,36,1024]{3,1,2,0:T(8,128)(2,1)S(1)}, u32[]{:S(2)}, u32[]{:S(2)}) %all-to-all-start.1) | async-done | bytes 2359328 | tf_op jit(solution)/shard_map/all_to_all | solution.py:91
  286.2 5.3 gather_fusion.1
  295.2 34.5 %all-reduce = f32[1024]{0:T(1024)S(1)} all-reduce(f32[1024]{0:T(1024)S(1)} %broadcast_multiply_fusion), channel_id=2, replica_groups=mesh['groups'=2,'expert'=4,'dp'=4] {'expert','dp'}, use_global_device_ids=true, to_apply=%region_11.12.clone | all-reduce | flops 1024 | bytes 8192
  337.3 105.1 %reduce-scatter.7.cloned.1.call-done = bf16[8,256,512]{2,1,0:T(8,128)(2,1)} async-done(((bf16[8,1024,512]{2,1,0:T(8,128)(2,1)}), bf16[8,256,512]{2,1,0:T(8,128)(2,1)}) %reduce-scatter.7.cloned.1.call-update) | async-done | bytes 2097168 | tf_op jit(solution)/shard_map/reduce_scatter | solution.py:98
  446.6 143.3 %reduce-scatter.9.cloned.1.call-done = bf16[8,256,512]{2,1,0:T(8,128)(2,1)} async-done(((bf16[8,1024,512]{2,1,0:T(8,128)(2,1)}), bf16[8,256,512]{2,1,0:T(8,128)(2,1)}) %reduce-scatter.9.cloned.1.call-update) | async-done | bytes 2097168 | tf_op jit(solution)/shard_map/reduce_scatter | solution.py:101
  594.1 73.3 %reduce-scatter.13.cloned.1.call-done = f32[64,1024]{1,0:T(8,128)} async-done(((f32[1024,1024]{1,0:T(8,128)}), f32[64,1024]{1,0:T(8,128)}) %reduce-scatter.13.cloned.1.call-update) | async-done | bytes 262160
  (91 shorter events, 96.2 us)
Async XLA Ops:
  7.2 224.1 %copy-start = (bf16[128,1024]{1,0:T(8,128)(2,1)S(1)}, bf16[128,1024]{1,0:T(8,128)(2,1)}, u32[]{:S(2)}) copy-start(bf16[128,1024]{1,0:T(8,128)(2,1)} %param.10) | copy-start | bytes 786436
  7.2 27.7 %copy-start.2 = (bf16[128,1024]{1,0:T(8,128)(2,1)S(1)}, bf16[128,1024]{1,0:T(8,128)(2,1)}, u32[]{:S(2)}) copy-start(bf16[128,1024]{1,0:T(8,128)(2,1)} %param.9) | copy-start | bytes 786436
  7.2 27.7 %copy-start.9 = (f32[1024]{0:T(1024)S(1)}, f32[1024]{0:T(1024)}, u32[]{:S(2)}) copy-start(f32[1024]{0:T(1024)} %param.11) | copy-start | bytes 12292
  59.5 32.7 %all-to-all-start = ((bf16[4,8,36,1024]{3,1,2,0:T(8,128)(2,1)}), bf16[4,8,36,1024]{3,1,2,0:T(8,128)(2,1)S(1)}, u32[]{:S(2)}, u32[]{:S(2)}) async-start(bf16[4,8,36,1024]{3,1,2,0:T(8,128)(2,1)} %copy.39), calls=%async_computation | async-start | bytes 4718592 | tf_op jit(solution)/shard_map/all_to_all | solution.py:89
  92.2 33.1 %all-to-all-start.2 = ((bf16[4,8,36,1024]{3,1,2,0:T(8,128)(2,1)}), bf16[4,8,36,1024]{3,1,2,0:T(8,128)(2,1)}, u32[]{:S(2)}, u32[]{:S(2)}) async-start(bf16[4,8,36,1024]{3,1,2,0:T(8,128)(2,1)} %copy.45), calls=%async_computation.2 | async-start | bytes 4718592 | tf_op jit(solution)/shard_map/all_to_all | solution.py:92
  96.7 236.5 %reduce-scatter.11.cloned.1.call-start = ((), (), s32[]{:S(2)}) async-start(), calls=%async_computation.10 | async-start | bytes 10485760 | tf_op jit(solution)/shard_map/reduce_scatter | solution.py:104
  137.2 1.1 copy-start.5
  148.1 294.3 %reduce-scatter.7.cloned.1.call-start = ((), (), s32[]{:S(2)}) async-start(), calls=%async_computation.8 | async-start | bytes 10485760 | tf_op jit(solution)/shard_map/reduce_scatter | solution.py:98
  158.1 431.8 %reduce-scatter.9.cloned.1.call-start = ((), (), s32[]{:S(2)}) async-start(), calls=%async_computation.9 | async-start | bytes 10485760 | tf_op jit(solution)/shard_map/reduce_scatter | solution.py:101
  168.2 1.3 copy-start.4
  169.5 6.4 copy-start.7
  184.9 32.1 %all-to-all-start.3 = ((bf16[4,8,36,1024]{3,1,2,0:T(8,128)(2,1)}), bf16[4,8,36,1024]{3,1,2,0:T(8,128)(2,1)S(1)}, u32[]{:S(2)}, u32[]{:S(2)}) async-start(bf16[4,8,36,1024]{3,1,2,0:T(8,128)(2,1)} %copy.47), calls=%async_computation.3 | async-start | bytes 4718592 | tf_op jit(solution)/shard_map/all_to_all | solution.py:96
  188.5 478.9 %reduce-scatter.13.cloned.1.call-start = ((), (), s32[]{:S(2)}) async-start(), calls=%async_computation.11 | async-start | bytes 4456448
  227.9 3.1 copy-start.3
  227.9 3.4 copy-start.8
  239.5 1.3 copy-start.6
  248.5 3.8 copy-start.10
  248.5 32.2 %all-to-all-start.1 = ((bf16[4,8,36,1024]{3,1,2,0:T(8,128)(2,1)}), bf16[4,8,36,1024]{3,1,2,0:T(8,128)(2,1)S(1)}, u32[]{:S(2)}, u32[]{:S(2)}) async-start(bf16[4,8,36,1024]{3,1,2,0:T(8,128)(2,1)} %copy.42), calls=%async_computation.1 | async-start | bytes 4718592 | tf_op jit(solution)/shard_map/all_to_all | solution.py:91
  291.6 38.7 %copy-start.1 = (bf16[1024,1024]{1,0:T(8,128)(2,1)S(1)}, bf16[1024,1024]{1,0:T(8,128)(2,1)}, u32[]{:S(2)}) copy-start(bf16[1024,1024]{1,0:T(8,128)(2,1)} %gather_fusion.1) | copy-start | bytes 6291460
Sparse Core Ops, SparseCore 0:
  148.2 145.6 reduce-scatter.10
  296.2 146.1 reduce-scatter.6
  444.8 145.1 reduce-scatter.8
  594.2 73.1 reduce-scatter.12
where the time goes:
time: 683 us; the launch traced here: 674 us
  waiting for transfers between devices  413 us (60%)
  matrix products  81.5 us (12%)
  local copies, waits for them, and re-layouts  78.5 us (11%)
  other arithmetic  34.8 us (5%)
  blocking collectives  34.5 us (5%)
  starting transfers between devices  17.3 us (3%)
  between operations  15.2 us (2%)
    reduce_scatter x1, waiting for transfers between devices, body(): lax.psum_scatter(up_term.astype(jnp.bfloat16), 'dp', scatter_dimension=1,...  143 us
    reduce_scatter x1, waiting for transfers between devices, body(): lax.psum_scatter(gate_term.astype(jnp.bfloat16), 'dp', scatter_dimension=...  105 us
    unnamed x5, waiting for transfers between devices  73.4 us
    unnamed x1, blocking collectives  34.5 us
    all_to_all x1, waiting for transfers between devices, body(): lax.all_to_all(input_delta, 'expert', split_axis=0, concat_axis=0, tiled=...  28.2 us
    all_to_all x1, waiting for transfers between devices, body(): lax.all_to_all(result, 'expert', split_axis=0, concat_axis=0, tiled=True)  27.2 us
    all_to_all x1, waiting for transfers between devices, body(): lax.all_to_all(send_in, 'expert', split_axis=0, concat_axis=0, tiled=True)  24.1 us
  transfers between devices with their start and end apart: 8, of which 7 were waited for; matrix products, arithmetic and copies ran while one was open for 17% of the time, Pallas kernels for 0%

commit v1 on v0

--- a/solution.py
+++ b/solution.py
@@ -48,7 +48,7 @@
     return (input_delta, gate_term, up_term, down_term)
 
 
-def body(hidden_in, context, norm_gain, route_ids, route_weights, w_gate, w_up, w_down, out_grad):
+def scattered_body(hidden_in, context, norm_gain, route_ids, route_weights, w_gate, w_up, w_down, out_grad):
     tok_rows = hidden_in.shape[0]
     feature_count = hidden_in.shape[1]
     top_count = route_ids.shape[1]
@@ -133,6 +133,125 @@
     return (moe_out, branch_grad, route_grad, gain_grad, proj_grad, gate_grad, up_grad, down_grad)
 
 
+def token_rows(ids, local_experts, capacity, first_expert):
+    blocks, owners, tok_rows, _ = ids.shape
+    named = first_expert + jnp.arange(local_experts, dtype=jnp.int32)
+    hit = jnp.any(ids[..., None] == named, axis=3)
+    order = jnp.arange(tok_rows)
+    before = (order[:, None] > order[None, :]).astype(jnp.bfloat16)
+    position = jnp.einsum(
+        "ut,sbtj->sbuj", before, hit.astype(jnp.bfloat16), preferred_element_type=jnp.float32
+    ).astype(jnp.int32)
+    base = jnp.arange(owners, dtype=jnp.int32)[None, :, None, None] * capacity
+    row = jnp.where(hit, base + position, -1)
+    return row.reshape(blocks, owners * tok_rows, local_experts)
+
+
+def gathered_body(hidden_in, context, norm_gain, route_ids, route_weights, w_gate, w_up, w_down, out_grad):
+    tok_rows, feature_count = hidden_in.shape
+    top_count = route_ids.shape[1]
+    local_experts, _, hidden_units = w_gate.shape
+    owners, parts = lax.axis_size("expert"), lax.axis_size("dp")
+    expert_at, part_at = lax.axis_index("expert"), lax.axis_index("dp")
+    capacity = tok_rows * top_count * 9 // (8 * local_experts * owners)
+    token_total = tok_rows * owners * parts
+    grad_scale = 8.0 / math.sqrt(token_total)
+    super_toks, super_rows = owners * tok_rows, owners * capacity
+    hidden = hidden_in.astype(jnp.float32)
+    inv_rms = lax.rsqrt(jnp.mean(hidden * hidden, axis=-1, keepdims=True) + EPSILON)
+    normed = hidden * inv_rms
+    scaled_in = (normed * norm_gain).astype(jnp.bfloat16)
+
+    def everywhere(block):
+        got = lax.all_gather(block, ("dp", "expert"), axis=0, tiled=True)
+        return got.reshape(parts, super_toks, block.shape[1])
+
+    routes = everywhere(jnp.concatenate([route_ids.astype(jnp.float32), route_weights], axis=1))
+    tok_in = everywhere(scaled_in)
+    tok_grad = everywhere(out_grad)
+    ids = routes[..., :top_count].astype(jnp.int32)
+    weights = routes[..., top_count:]
+    first_expert = expert_at * local_experts
+    row = token_rows(
+        ids.reshape(parts, owners, tok_rows, top_count), local_experts, capacity, first_expert
+    )
+    named = first_expert + jnp.arange(local_experts, dtype=jnp.int32)
+    match = ids[..., None] == named
+    tok_weight = jnp.sum(jnp.where(match, weights[..., None], 0.0), axis=2)
+    slots = jnp.arange(super_rows, dtype=jnp.int32)
+    pick_mask = row.transpose(2, 0, 1)[:, :, None, :] == slots[:, None]
+    pick = pick_mask.astype(jnp.bfloat16)
+    slot_weight = jnp.sum(
+        jnp.where(pick_mask, tok_weight.transpose(2, 0, 1)[:, :, None, :], 0.0), axis=-1
+    )
+    rows_in = jnp.einsum(
+        "jsct,std->jscd", pick, tok_in, preferred_element_type=jnp.float32
+    ).astype(jnp.bfloat16)
+    raw_grad = jnp.einsum("jsct,std->jscd", pick, tok_grad, preferred_element_type=jnp.float32)
+    rows_grad = (slot_weight[..., None] * raw_grad).astype(jnp.bfloat16)
+    flat = (local_experts, parts * super_rows)
+    rows_in = rows_in.reshape(*flat, feature_count)
+    rows_grad = rows_grad.reshape(*flat, feature_count)
+    dot = lambda spec, a, b: jnp.einsum(spec, a, b, preferred_element_type=jnp.float32)
+    gate_pre = dot("jrd,jdf->jrf", rows_in, w_gate)
+    up_pre = dot("jrd,jdf->jrf", rows_in, w_up)
+    hidden_act = (jax.nn.silu(gate_pre) * up_pre).astype(jnp.bfloat16)
+    inner_grad = dot("jrd,jfd->jrf", rows_grad, w_down)
+    gate_delta = (inner_grad * up_pre * silu_slope(gate_pre)).astype(jnp.bfloat16)
+    up_delta = (inner_grad * jax.nn.silu(gate_pre)).astype(jnp.bfloat16)
+
+    def own(rows):
+        return lax.dynamic_slice_in_dim(rows, part_at * super_rows, super_rows, axis=1)
+
+    own_pick = lax.dynamic_index_in_dim(pick, part_at, axis=1, keepdims=False)
+    own_weight = lax.dynamic_index_in_dim(tok_weight, part_at, axis=0, keepdims=False)
+    own_match = lax.dynamic_index_in_dim(match, part_at, axis=0, keepdims=False)
+    own_raw = lax.dynamic_index_in_dim(raw_grad, part_at, axis=1, keepdims=False)
+    result = dot("jcf,jfd->jcd", own(hidden_act), w_down).astype(jnp.bfloat16)
+    input_delta = (
+        dot("jcf,jdf->jcd", own(gate_delta), w_gate) + dot("jcf,jdf->jcd", own(up_delta), w_up)
+    ).astype(jnp.bfloat16)
+    weighted = own_pick * own_weight.T.astype(jnp.bfloat16)[:, None, :]
+    moe_term = dot("jct,jcd->td", weighted, result).astype(jnp.bfloat16)
+    delta_term = dot("jct,jcd->td", own_pick, input_delta).astype(jnp.bfloat16)
+    slot_route = jnp.sum(own_raw * result.astype(jnp.float32), axis=-1)
+    tok_route = jnp.sum(jnp.where(own_pick > 0, slot_route[..., None], 0.0), axis=1)
+    route_term = jnp.sum(jnp.where(own_match, tok_route.T[:, None, :], 0.0), axis=-1)
+    scatter = lambda term: lax.psum_scatter(term, "expert", scatter_dimension=0, tiled=True)
+    moe_out = scatter(moe_term)
+    norm_delta = scatter(delta_term).astype(jnp.float32)
+    route_grad = scatter(route_term)
+
+    cols, units = feature_count // parts, hidden_units // parts
+    cut_in = lax.dynamic_slice_in_dim(rows_in, part_at * cols, cols, axis=2)
+    cut_act = lax.dynamic_slice_in_dim(hidden_act, part_at * units, units, axis=2)
+    gate_grad = dot("jrd,jrf->jdf", cut_in, gate_delta) * grad_scale
+    up_grad = dot("jrd,jrf->jdf", cut_in, up_delta) * grad_scale
+    down_grad = dot("jrf,jrd->jfd", cut_act, rows_grad) * grad_scale
+
+    scaled_delta = norm_delta * norm_gain
+    branch = inv_rms * (
+        scaled_delta - normed * jnp.mean(scaled_delta * normed, axis=-1, keepdims=True)
+    )
+    branch_grad = branch.astype(jnp.bfloat16)
+    full_grad = (out_grad.astype(jnp.float32) + branch).astype(jnp.bfloat16)
+    proj_term = lax.dot_general(
+        context, full_grad, (((0,), (0,)), ((), ())), preferred_element_type=jnp.float32
+    ) / math.sqrt(token_total)
+    gain_term = jnp.sum(norm_delta * normed, axis=0) * grad_scale
+    everyone = lambda term: lax.psum_scatter(
+        term, ("expert", "dp"), scatter_dimension=0, tiled=True
+    )
+    proj_grad = everyone(proj_term.astype(jnp.bfloat16)).astype(jnp.float32)
+    gain_grad = everyone(gain_term)
+    return (moe_out, branch_grad, route_grad, gain_grad, proj_grad, gate_grad, up_grad, down_grad)
+
+
+def body(*args):
+    few = lax.axis_size("dp") <= 4 and lax.axis_size("expert") <= 4
+    return (gathered_body if few else scattered_body)(*args)
+
+
 def solution(mesh):
     return jax.shard_map(
         body,

time: 683 us -> 347 us (0.51); the launches traced: 674 us -> 346 us
  waiting for transfers between devices: 413 us -> 115 us
  local copies, waits for them, and re-layouts: 78.5 us -> 24.2 us
  matrix products: 81.5 us -> 123 us
  other arithmetic: 34.8 us -> 12.9 us
  blocking collectives: 34.5 us -> 56.2 us
  starting transfers between devices: 17.3 us -> 0.5 us
    reduce_scatter x3, waiting for transfers between devices: 248 us -> 62.5 us  [gathered_body(): lax.psum_scatter(term, 'expert', scatter_dimension=0, tiled=True)]
    all_to_all x4 -> x0, waiting for transfers between devices: 90.8 us -> none  [the longest x1 28.2 us: body(): lax.all_to_all(input_delta, 'expert', split_axis=0, concat_axis=0, tiled=...]
    unnamed x5 -> x7, waiting for transfers between devices: 73.4 us -> 0.76 us
    all_gather x0 -> x2, waiting for transfers between devices: none -> 51.7 us  [everywhere(): got = lax.all_gather(block, ('dp', 'expert'), axis=0, tiled=True)]
    dot_general x11 -> x14, matrix products: 81.5 us -> 123 us  [the longest x10 96.8 us: gathered_body(): jnp.einsum(spec, a, b, preferred_element_type=jnp.float32)]
    gather x6 -> x0, local copies, waits for them, and re-layouts: 28.5 us -> none  [the longest x2 10.2 us: body(): out_grad32[slot_token]]
    all_gather x0 -> x1, blocking collectives: none -> 23.6 us  [everywhere(): got = lax.all_gather(block, ('dp', 'expert'), axis=0, tiled=True)]
    all_to_all x4 -> x0, starting transfers between devices: 16.1 us -> none  [the longest x1 4.54 us: body(): lax.all_to_all(send_grad, 'expert', split_axis=0, concat_axis=0, tiled=True)]
  transfers between devices with their start and end apart: 8 -> 6, of which waited for: 7 -> 5; matrix products, arithmetic and copies ran while one was open for 17% -> 20% of each run, Pallas kernels for 0% -> 0%
where the time goes in v1:
time: 347 us; the launch traced here: 346 us
  matrix products  123 us (35%)
  waiting for transfers between devices  115 us (33%)
  blocking collectives  56.2 us (16%)
  local copies, waits for them, and re-layouts  24.2 us (7%)
  between operations  15 us (4%)
  other arithmetic  12.9 us (4%)
    dot_general x10, matrix products, gathered_body(): jnp.einsum(spec, a, b, preferred_element_type=jnp.float32)  96.8 us
    reduce_scatter x3, waiting for transfers between devices, gathered_body(): lax.psum_scatter(term, 'expert', scatter_dimension=0, tiled=True)  62.5 us
    all_gather x2, waiting for transfers between devices, everywhere(): got = lax.all_gather(block, ('dp', 'expert'), axis=0, tiled=True)  51.7 us
    unnamed x1, blocking collectives  32.6 us
    all_gather x1, blocking collectives, everywhere(): got = lax.all_gather(block, ('dp', 'expert'), axis=0, tiled=True)  23.6 us
    dot_general x1, matrix products, gathered_body(): jnp.einsum('jsct,std->jscd', pick, tok_grad, preferred_element_type=jnp.f...  14.4 us
    dot_general x1, matrix products, gathered_body(): jnp.einsum('jsct,std->jscd', pick, tok_in, preferred_element_type=jnp.flo...  9.52 us
    convert_element_type x1, local copies, waits for them, and re-layouts, gathered_body(): rows_grad = (slot_weight[..., None] * raw_grad).astype(jnp.bfloat16)  9.24 us
  transfers between devices with their start and end apart: 6, of which 5 were waited for; matrix products, arithmetic and copies ran while one was open for 20% of the time, Pallas kernels for 0%

profile of v1, /device:TPU:0, one launch (start us, length us, event | category | flops | bytes accessed | tf_op | source)
XLA Modules:
  0.0 346.4 jit_solution(10354257931461635538)
XLA Ops:
  12.3 23.6 %all_gather.9 = f32[2048,16]{0,1:T(8,128)S(1)} all-gather(f32[128,16]{0,1:T(8,128)S(1)} %pad_maximum_fusion), channel_id=1, replica_groups=mesh['groups'=2,'expert'=4,'dp'=4] {'dp','expert'}, dimensions={0}, use_global_device_ids=true | all-gather | bytes 139264 | tf_op jit(solution)/shard_map/all_gather | solution.py:166
  37.8 2.6 iota_compare_fusion
  40.4 23.4 %all-gather.5.cloned.1.call-done = bf16[2048,1024]{1,0:T(8,128)(2,1)} async-done(((bf16[128,1024]{1,0:T(8,128)(2,1)}), bf16[2048,1024]{1,0:T(8,128)(2,1)}) %all-gather.5.cloned.1.call-update) | async-done | bytes 4194320 | tf_op jit(solution)/shard_map/all_gather | solution.py:166
  63.8 14.4 %fusion = (bf16[8,4,144,1024]{3,2,0,1:T(8,128)(2,1)}, f32[4,8,144,1024]{3,2,1,0:T(8,128)}) fusion(f32[8,4,144]{2,0,1:T(8,128)S(1)} %select_reduce_fusion, bf16[4,512,1024,1]{2,1,3,0:T(8,128)(2,1)} %bitcast.94, s32[8,4,512]{2,0,1:T(8,128)S(1)} %fusion.29), kind=kOutput, calls=%fused_computation.1 | convolution fusion | flops 4843634688 | bytes 32589824 | tf_op jit(solution)/shard_map/jsct,std->jscd/dot_general | solution.py:190
  78.2 9.2 %copy.51 = bf16[8,4,144,1024]{3,2,1,0:T(8,128)(2,1)} copy(bf16[8,4,144,1024]{3,2,0,1:T(8,128)(2,1)} %get-tuple-element.73) | data formatting | bytes 18874368 | tf_op jit(solution)/shard_map/convert_element_type | solution.py:191
  87.4 28.3 %all-gather.3.cloned.1.call-done = bf16[2048,1024]{1,0:T(8,128)(2,1)} async-done(((bf16[128,1024]{1,0:T(8,128)(2,1)}), bf16[2048,1024]{1,0:T(8,128)(2,1)}) %all-gather.3.cloned.1.call-update) | async-done | bytes 4194320 | tf_op jit(solution)/shard_map/all_gather | solution.py:166
  115.8 9.5 %convert_bitcast_fusion = bf16[8,4,144,1024]{3,2,0,1:T(8,128)(2,1)} fusion(bf16[4,512,1024,1]{2,1,3,0:T(8,128)(2,1)} %bitcast.97, s32[8,4,512]{2,0,1:T(8,128)S(1)} %fusion.29), kind=kOutput, calls=%fused_computation.8 | convolution fusion | flops 4838916096 | bytes 13697024 | tf_op jit(solution)/shard_map/jsct,std->jscd/dot_general | solution.py:187
  125.3 9.1 %copy.50 = bf16[8,4,144,1024]{3,2,1,0:T(8,128)(2,1)} copy(bf16[8,4,144,1024]{3,2,0,1:T(8,128)(2,1)} %convert_bitcast_fusion) | data formatting | bytes 18874368 | tf_op jit(solution)/shard_map/convert_element_type | solution.py:189
  134.4 12.3 %fusion.57 = f32[8,576,512]{2,1,0:T(8,128)} fusion(bf16[8,576,1024]{2,1,0:T(8,128)(2,1)} %bitcast.90, bf16[8,1024,512]{2,1,0:T(8,128)(2,1)} %param.14), kind=kOutput, calls=%fused_computation.88 | convolution fusion | flops 4831838208 | bytes 27262976 | tf_op jit(solution)/shard_map/jrd,jdf->jrf/dot_general | solution.py:195
  146.7 10.7 %fusion.58 = f32[8,576,512]{2,1,0:T(8,128)} fusion(bf16[8,576,1024]{2,1,0:T(8,128)(2,1)S(1)} %bitcast.93, bf16[8,1024,512]{2,1,0:T(8,128)(2,1)} %param.15), kind=kOutput, calls=%fused_computation.89 | convolution fusion | flops 4831838208 | bytes 27262976 | tf_op jit(solution)/shard_map/jrd,jdf->jrf/dot_general | solution.py:195
  157.4 22.4 %multiply_convert_fusion = (bf16[8,576,512]{2,1,0:T(8,128)(2,1)}, bf16[8,576,512]{2,1,0:T(8,128)(2,1)}, bf16[8,576,512]{2,1,0:T(8,128)(2,1)}) fusion(f32[8,576,512]{2,1,0:T(8,128)} %fusion.57, f32[8,576,512]{2,1,0:T(8,128)} %fusion.58, bf16[8,576,1024]{2,1,0:T(8,128)(2,1)} %bitcast.86, bf16[8,512,1024]{2,1,0:T(8,128)(2,1)} %param.16), kind=kOutput, calls=%fused_computation.2 | convolution fusion | flops 4867227648 | bytes 50855936 | tf_op jit(solution)/shard_map/jrd,jfd->jrf/dot_general | solution.py:195
  179.9 8.8 %fusion.23 = f32[8,144,1024]{2,1,0:T(8,128)} fusion(bf16[8,1024,512]{2,1,0:T(8,128)(2,1)} %param.14, bf16[8,576,512]{2,1,0:T(8,128)(2,1)} %get-tuple-element.67, s32[]{:T(128)S(6)} %select_n.44), kind=kOutput, calls=%fused_computation.37 | convolution fusion | flops 1207959552 | bytes 14286852 | tf_op jit(solution)/shard_map/jcf,jdf->jcd/dot_general | solution.py:195
  188.7 10.5 %bitcast_convert_fusion = bf16[512,1024]{1,0:T(8,128)(2,1)} fusion(f32[8,144,1024]{2,1,0:T(8,128)} %fusion.23, pred[8,4,144,512]{3,2,0,1:T(8,128)(4,1)} %iota_compare_fusion, s32[]{:T(128)S(6)} %select_n.42, bf16[8,1024,512]{2,1,0:T(8,128)(2,1)} %param.15, bf16[8,576,512]{2,1,0:T(8,128)(2,1)} %get-tuple-element.66, s32[]{:T(128)S(6)} %select_n.44), kind=kOutput, calls=%fused_computation.24 | convolution fusion | flops 2418802688 | bytes 15925256 | tf_op jit(solution)/shard_map/jct,jcd->td/dot_general | solution.py:195
  199.3 23.5 %reduce-scatter.9.cloned.1.call-done = bf16[128,1024]{1,0:T(8,128)(2,1)} async-done(((bf16[512,1024]{1,0:T(8,128)(2,1)}), bf16[128,1024]{1,0:T(8,128)(2,1)}) %reduce-scatter.9.cloned.1.call-update) | async-done | bytes 262160 | tf_op jit(solution)/shard_map/reduce_scatter | solution.py:220
  224.0 1.8 fusion.12
  225.8 2.6 copy.56
  228.6 8.0 %fusion.4 = (f32[8,144]{1,0:T(8,128)S(1)}, bf16[8,144,1024]{2,1,0:T(8,128)(2,1)}) fusion(f32[4,8,144,1024]{3,2,1,0:T(8,128)} %get-tuple-element.74, s32[]{:T(128)S(6)} %select_n.42, bf16[8,512,1024]{2,1,0:T(8,128)(2,1)} %param.16, bf16[8,576,512]{2,1,0:T(8,128)(2,1)} %get-tuple-element.68, s32[]{:T(128)S(6)} %select_n.44), kind=kOutput, calls=%fused_computation.13 | convolution fusion | flops 1212676992 | bytes 16650760 | tf_op jit(solution)/shard_map/jcf,jfd->jcd/dot_general | solution.py:195
  239.1 4.5 %bitcast_convert_fusion.1 = bf16[512,1024]{1,0:T(8,128)(2,1)} fusion(bf16[8,144,1024]{2,1,0:T(8,128)(2,1)} %get-tuple-element.76, pred[8,4,144,512]{3,2,0,1:T(8,128)(4,1)} %iota_compare_fusion, s32[]{:T(128)S(6)} %select_n.42, bf16[8,512]{1,0:T(8,128)(2,1)S(1)} %fusion.46), kind=kOutput, calls=%fused_computation.25 | convolution fusion | flops 1209663488 | bytes 4005892 | tf_op jit(solution)/shard_map/jct,jcd->td/dot_general | solution.py:195
  244.9 7.2 %convolution_multiply_fusion = f32[8,256,512]{2,1,0:T(8,128)} fusion(bf16[8,576,512]{2,1,0:T(8,128)(2,1)} %get-tuple-element.66, bf16[8,576,1024]{2,1,0:T(8,128)(2,1)} %bitcast.91, s32[]{:T(128)S(6)} %select_n.48), kind=kOutput, calls=%fused_computation.21 | convolution fusion | flops 1209008128 | bytes 11272196 | tf_op jit(solution)/shard_map/jrd,jrf->jdf/dot_general | solution.py:195
  252.1 7.0 %convolution_multiply_fusion.1 = f32[8,256,512]{2,1,0:T(8,128)} fusion(bf16[8,576,512]{2,1,0:T(8,128)(2,1)} %get-tuple-element.67, bf16[8,576,1024]{2,1,0:T(8,128)(2,1)} %bitcast.92, s32[]{:T(128)S(6)} %select_n.48), kind=kOutput, calls=%fused_computation.22 | convolution fusion | flops 1209008128 | bytes 11272196 | tf_op jit(solution)/shard_map/jrd,jrf->jdf/dot_general | solution.py:195
  259.2 5.3 %convolution_multiply_fusion.2 = f32[8,128,1024]{2,1,0:T(8,128)} fusion(bf16[8,576,1024]{2,1,0:T(8,128)(2,1)S(1)} %bitcast.89, bf16[8,576,512]{2,1,0:T(8,128)(2,1)} %get-tuple-element.68, s32[]{:T(128)S(6)} %select_n.49), kind=kOutput, calls=%fused_computation.23 | convolution fusion | flops 1209008128 | bytes 14811140 | tf_op jit(solution)/shard_map/jrf,jrd->jfd/dot_general | solution.py:195
  264.5 32.6 %all-reduce = f32[1024]{0:T(1024)S(1)} all-reduce(f32[1024]{0:T(1024)S(1)} %broadcast_multiply_fusion), channel_id=5, replica_groups=mesh['groups'=2,'expert'=4,'dp'=4] {'expert','dp'}, use_global_device_ids=true, to_apply=%region_12.13.clone | all-reduce | flops 1024 | bytes 8192
  300.5 11.0 %reduce-scatter.11.cloned.1.call-done = f32[128,8]{0,1:T(8,128)} async-done(((f32[512,8]{0,1:T(8,128)}), f32[128,8]{0,1:T(8,128)}) %reduce-scatter.11.cloned.1.call-update) | async-done | bytes 4112 | tf_op jit(solution)/shard_map/reduce_scatter | solution.py:220
  311.5 28.0 %reduce-scatter.7.cloned.1.call-done = bf16[128,1024]{1,0:T(8,128)(2,1)} async-done(((bf16[512,1024]{1,0:T(8,128)(2,1)}), bf16[128,1024]{1,0:T(8,128)(2,1)}) %reduce-scatter.7.cloned.1.call-update) | async-done | bytes 262160 | tf_op jit(solution)/shard_map/reduce_scatter | solution.py:220
  (61 shorter events, 14.9 us)
Async XLA Ops:
  7.2 216.8 %copy-start = (bf16[128,1024]{1,0:T(8,128)(2,1)S(1)}, bf16[128,1024]{1,0:T(8,128)(2,1)}, u32[]{:S(2)}) copy-start(bf16[128,1024]{1,0:T(8,128)(2,1)} %param.10) | copy-start | bytes 786436
  7.2 56.6 %all-gather.5.cloned.1.call-start = ((), (), s32[]{:S(2)}) async-start(), calls=%async_computation.6 | async-start | bytes 4456448 | tf_op jit(solution)/shard_map/all_gather | solution.py:166
  7.9 107.8 %all-gather.3.cloned.1.call-start = ((), (), s32[]{:S(2)}) async-start(), calls=%async_computation.4 | async-start | bytes 4456448 | tf_op jit(solution)/shard_map/all_gather | solution.py:166
  10.9 211.9 %reduce-scatter.9.cloned.1.call-start = ((), (), s32[]{:S(2)}) async-start(), calls=%async_computation.7 | async-start | bytes 1310720 | tf_op jit(solution)/shard_map/reduce_scatter | solution.py:220
  134.4 12.3 %copy-start.1 = (bf16[8,4,144,1024]{3,2,1,0:T(8,128)(2,1)S(1)}, bf16[8,4,144,1024]{3,2,1,0:T(8,128)(2,1)}, u32[]{:S(2)}) copy-start(bf16[8,4,144,1024]{3,2,1,0:T(8,128)(2,1)} %copy.50) | copy-start | bytes 28311556
  188.6 34.1 %copy-start.2 = (bf16[128,1024]{1,0:T(8,128)(2,1)S(1)}, bf16[128,1024]{1,0:T(8,128)(2,1)}, u32[]{:S(2)}) copy-start(bf16[128,1024]{1,0:T(8,128)(2,1)} %param.9) | copy-start | bytes 786436
  188.6 34.1 %copy-start.5 = (f32[1024]{0:T(1024)S(1)}, f32[1024]{0:T(1024)}, u32[]{:S(2)}) copy-start(f32[1024]{0:T(1024)} %param.11) | copy-start | bytes 12292
  188.6 35.3 %copy-start.4 = (bf16[128,1024]{1,0:T(8,128)(2,1)S(1)}, bf16[128,1024]{1,0:T(8,128)(2,1)}, u32[]{:S(2)}) copy-start(bf16[128,1024]{1,0:T(8,128)(2,1)} %param.17) | copy-start | bytes 786436
  199.2 99.4 %reduce-scatter.13.cloned.1.call-start = ((), (), s32[]{:S(2)}) async-start(), calls=%async_computation.9 | async-start | bytes 2228224
  228.4 83.1 %reduce-scatter.11.cloned.1.call-start = ((), (), s32[]{:S(2)}) async-start(), calls=%async_computation.8 | async-start | bytes 20480 | tf_op jit(solution)/shard_map/reduce_scatter | solution.py:220
  236.6 7.0 %copy-start.6 = (u32[32]{0:T(128)S(1)}, u32[32]{0:T(128)}, u32[]{:S(2)}) copy-start(u32[32]{0:T(128)} %constant.70) | copy-start | bytes 388
  238.8 100.7 %reduce-scatter.7.cloned.1.call-start = ((), (), s32[]{:S(2)}) async-start(), calls=%async_computation.5 | async-start | bytes 1310720 | tf_op jit(solution)/shard_map/reduce_scatter | solution.py:220
  244.9 14.3 %slice-start = ((s8[9437184]{0:T(1024)(128)(4,1)}), s8[4194304]{0:T(1024)(128)(4,1)S(1)}, s32[]{:S(2)}) async-start(s8[9437184]{0:T(1024)(128)(4,1)} %bitcast.87), calls=%async_computation.10 | async-start | bytes 8388608
  244.9 14.3 %slice-start.1 = ((s8[9437184]{0:T(1024)(128)(4,1)}), s8[4194304]{0:T(1024)(128)(4,1)S(1)}, s32[]{:S(2)}) async-start(s8[9437184]{0:T(1024)(128)(4,1)} %bitcast.87), calls=%async_computation.11 | async-start | bytes 8388608
  252.1 7.1 %slice-start.2 = ((s8[9437184]{0:T(1024)(128)(4,1)}), s8[1048576]{0:T(1024)(128)(4,1)S(1)}, s32[]{:S(2)}) async-start(s8[9437184]{0:T(1024)(128)(4,1)} %bitcast.87), calls=%async_computation.12 | async-start | bytes 2097152
  259.2 38.5 %copy-start.3 = (bf16[128,1024]{1,0:T(8,128)(2,1)S(1)}, bf16[128,1024]{1,0:T(8,128)(2,1)}, u32[]{:S(2)}) copy-start(bf16[128,1024]{1,0:T(8,128)(2,1)} %reduce-scatter.9.cloned.1.call-done) | copy-start | bytes 786436
Sparse Core Ops, SparseCore 0:
  10.2 53.5 all-gather.4
  66.5 49.2 all-gather.2
  199.3 23.3 reduce-scatter.8
  228.5 61.5 reduce-scatter.12
  293.0 18.4 reduce-scatter.10
  314.6 24.8 reduce-scatter.6

commit v2 on v1

--- a/solution.py
+++ b/solution.py
@@ -3,6 +3,8 @@
 import jax
 import jax.numpy as jnp
 from jax import lax
+from jax.experimental import pallas as pl
+from jax.experimental.pallas import tpu as pltpu
 from jax.sharding import PartitionSpec as P
 
 EPSILON = 1e-05
@@ -133,6 +135,141 @@
     return (moe_out, branch_grad, route_grad, gain_grad, proj_grad, gate_grad, up_grad, down_grad)
 
 
+def spread_kernel(a_in, b_in, a_all, b_all, own_sem, send_sem, recv_sem):
+    parts, owners = a_all.shape[:2]
+    at, line = lax.axis_index("expert"), lax.axis_index("dp")
+    sibling = at + 1 - 2 * lax.rem(at, 2)
+    across = lax.rem(at + 2, owners)
+    sibling_across = lax.rem(sibling + 2, owners)
+    below, above = line > 0, line < parts - 1
+    always = line >= 0
+    partner = {
+        "across": (across, line, always),
+        "above": (at, line + 1, above),
+        "below": (at, line - 1, below),
+        "sibling": (sibling, line, always),
+    }
+    names = list(partner)
+    barrier = pltpu.get_barrier_semaphore()
+    for name in names:
+        to, to_line, cond = partner[name]
+
+        @pl.when(cond)
+        def _():
+            pl.semaphore_signal(
+                barrier,
+                inc=1,
+                device_id={"expert": to, "dp": to_line},
+                device_id_type=pl.DeviceIdType.MESH,
+            )
+
+    neighbours = lax.div(line + parts - 1, parts) + lax.div(2 * parts - 2 - line, parts)
+    pl.semaphore_wait(barrier, 2 + neighbours)
+
+    buffers = (a_all, b_all)
+    started = []
+
+    def copy(which, of, of_line, name, source):
+        to, to_line, _ = partner[name]
+        place = buffers[which].at[of_line, of]
+        return pltpu.make_async_remote_copy(
+            src_ref=place if source is None else source,
+            dst_ref=place,
+            send_sem=send_sem.at[which, of_line, of, names.index(name)],
+            recv_sem=recv_sem.at[which, of_line, of],
+            device_id={"expert": to, "dp": to_line},
+            device_id_type=pl.DeviceIdType.MESH,
+        )
+
+    def push(which, of, of_line, there, name, source=None):
+        cond = jnp.logical_and(there, partner[name][2])
+
+        @pl.when(cond)
+        def _():
+            copy(which, of, of_line, name, source).start()
+
+        started.append((which, of, of_line, cond, name, source))
+
+    def arrived(which, of, of_line, there):
+        @pl.when(there)
+        def _():
+            copy(which, of, of_line, "sibling", None).wait_recv()
+
+    def relay(which, of, of_line, there, targets):
+        arrived(which, of, of_line, there)
+        for name in targets:
+            push(which, of, of_line, there, name)
+
+    mine = [
+        pltpu.make_async_copy(source, buffer.at[line, at], own_sem.at[i])
+        for i, (source, buffer) in enumerate(((a_in, a_all), (b_in, b_all)))
+    ]
+    for name in ("above", "below", "across", "sibling"):
+        push(0, at, line, always, name, a_in)
+        push(1, at, line, always, name, b_in)
+    for copy_in in mine:
+        copy_in.start()
+    for step in range(1, parts + 1):
+        low, high = line - step, line + step
+        has_low, has_high = low >= 0, high < parts
+        low1, high1 = line - (step - 1), line + (step - 1)
+        has_low1, has_high1 = low1 >= 0, high1 < parts
+        if step < parts:
+            relay(0, at, low, has_low, ("above", "across", "sibling"))
+            relay(0, at, high, has_high, ("below", "across", "sibling"))
+        if step == 1:
+            relay(1, across, line, always, ("above", "below", "sibling"))
+        else:
+            relay(1, across, low1, has_low1, ("above", "sibling"))
+            relay(1, across, high1, has_high1, ("below", "sibling"))
+        if step < parts:
+            relay(1, at, low, has_low, ("above", "sibling"))
+            relay(1, at, high, has_high, ("below", "sibling"))
+        if step == 1:
+            relay(0, across, line, always, ("sibling",))
+        else:
+            relay(0, across, low1, has_low1, ("sibling",))
+            relay(0, across, high1, has_high1, ("sibling",))
+    for of_line in range(parts):
+        for of in (sibling, sibling_across):
+            for which in range(2):
+                arrived(which, of, of_line, always)
+    for which, of, of_line, cond, name, source in started:
+
+        @pl.when(cond)
+        def _():
+            copy(which, of, of_line, name, source).wait_send()
+
+    for copy_in in mine:
+        copy_in.wait()
+
+
+def spread(a_block, b_block, parts, owners):
+    any_space = pl.BlockSpec(memory_space=pl.ANY)
+    return pl.pallas_call(
+        spread_kernel,
+        out_shape=[
+            jax.ShapeDtypeStruct((parts, owners, *block.shape), block.dtype)
+            for block in (a_block, b_block)
+        ],
+        in_specs=[any_space, any_space],
+        out_specs=[any_space, any_space],
+        scratch_shapes=[
+            pltpu.SemaphoreType.DMA((2,)),
+            pltpu.SemaphoreType.DMA((2, parts, owners, 4)),
+            pltpu.SemaphoreType.DMA((2, parts, owners)),
+        ],
+        compiler_params=pltpu.CompilerParams(collective_id=0, has_side_effects=True),
+    )(a_block, b_block)
+
+
+def three_terms(value):
+    high = lax.reduce_precision(value, 8, 7)
+    middle = lax.reduce_precision(value - high, 8, 7)
+    low = value - high - middle
+    return [term.astype(jnp.bfloat16) for term in (high, middle, low)]
+
+
 def token_rows(ids, local_experts, capacity, first_expert):
     blocks, owners, tok_rows, _ = ids.shape
     named = first_expert + jnp.arange(local_experts, dtype=jnp.int32)
@@ -162,15 +299,18 @@
     normed = hidden * inv_rms
     scaled_in = (normed * norm_gain).astype(jnp.bfloat16)
 
-    def everywhere(block):
-        got = lax.all_gather(block, ("dp", "expert"), axis=0, tiled=True)
-        return got.reshape(parts, super_toks, block.shape[1])
-
-    routes = everywhere(jnp.concatenate([route_ids.astype(jnp.float32), route_weights], axis=1))
-    tok_in = everywhere(scaled_in)
-    tok_grad = everywhere(out_grad)
-    ids = routes[..., :top_count].astype(jnp.int32)
-    weights = routes[..., top_count:]
+    routes = jnp.concatenate([route_ids.astype(jnp.bfloat16), *three_terms(route_weights)], axis=1)
+    routes = jnp.pad(routes, ((0, 0), (0, -routes.shape[1] % 128)))
+    tok_in, tok_grad = spread(
+        jnp.concatenate([scaled_in, routes], axis=1), out_grad, parts, owners
+    )
+    tok_in = tok_in.reshape(parts, super_toks, -1)
+    tok_grad = tok_grad.reshape(parts, super_toks, feature_count)
+    routes = tok_in[..., feature_count:].astype(jnp.float32)
+    tok_in = tok_in[..., :feature_count]
+    terms = [routes[..., i * top_count : (i + 1) * top_count] for i in range(4)]
+    ids = terms[0].astype(jnp.int32)
+    weights = terms[1] + terms[2] + terms[3]
     first_expert = expert_at * local_experts
     row = token_rows(
         ids.reshape(parts, owners, tok_rows, top_count), local_experts, capacity, first_expert
@@ -217,9 +357,14 @@
     slot_route = jnp.sum(own_raw * result.astype(jnp.float32), axis=-1)
     tok_route = jnp.sum(jnp.where(own_pick > 0, slot_route[..., None], 0.0), axis=1)
     route_term = jnp.sum(jnp.where(own_match, tok_route.T[:, None, :], 0.0), axis=-1)
-    scatter = lambda term: lax.psum_scatter(term, "expert", scatter_dimension=0, tiled=True)
-    moe_out = scatter(moe_term)
-    norm_delta = scatter(delta_term).astype(jnp.float32)
+
+    def scatter(term):
+        cut = term.reshape(owners, tok_rows, -1)
+        got = lax.all_to_all(cut, "expert", split_axis=0, concat_axis=0, tiled=True)
+        return jnp.sum(got.astype(jnp.float32), axis=0)
+
+    norm_delta = scatter(delta_term)
+    moe_out = scatter(moe_term).astype(jnp.bfloat16)
     route_grad = scatter(route_term)
 
     cols, units = feature_count // parts, hidden_units // parts
@@ -239,16 +384,18 @@
         context, full_grad, (((0,), (0,)), ((), ())), preferred_element_type=jnp.float32
     ) / math.sqrt(token_total)
     gain_term = jnp.sum(norm_delta * normed, axis=0) * grad_scale
-    everyone = lambda term: lax.psum_scatter(
-        term, ("expert", "dp"), scatter_dimension=0, tiled=True
-    )
-    proj_grad = everyone(proj_term.astype(jnp.bfloat16)).astype(jnp.float32)
-    gain_grad = everyone(gain_term)
+    gain_cols = jnp.stack(three_terms(gain_term), axis=1)
+    gain_cols = jnp.pad(gain_cols, ((0, 0), (0, 125)))
+    both = jnp.concatenate([proj_term.astype(jnp.bfloat16), gain_cols], axis=1)
+    both = lax.psum_scatter(both, ("expert", "dp"), scatter_dimension=0, tiled=True)
+    both = both.astype(jnp.float32)
+    proj_grad = both[:, :feature_count]
+    gain_grad = jnp.sum(both[:, feature_count:], axis=1)
     return (moe_out, branch_grad, route_grad, gain_grad, proj_grad, gate_grad, up_grad, down_grad)
 
 
 def body(*args):
-    few = lax.axis_size("dp") <= 4 and lax.axis_size("expert") <= 4
+    few = lax.axis_size("dp") <= 4 and lax.axis_size("expert") == 4
     return (gathered_body if few else scattered_body)(*args)
 
 

time: 347 us -> 290 us (0.84)
  waiting for transfers between devices: 115 us -> 24 us
  Pallas kernels: 0 us -> 61.4 us
  blocking collectives: 56.2 us -> 17.3 us
  starting transfers between devices: 0.5 us -> 6.81 us
  other arithmetic: 12.9 us -> 16.5 us
    reduce_scatter x3 -> x0, waiting for transfers between devices: 62.5 us -> none  [gathered_body(): lax.psum_scatter(term, 'expert', scatter_dimension=0, tiled=True)]
    pallas_call x0 -> x1, Pallas kernels: none -> 61.4 us  [spread(): pl.pallas_call(spread_kernel, out_shape=[jax.ShapeDtypeStruct((parts, own...]
    all_gather x2 -> x0, waiting for transfers between devices: 51.7 us -> none  [everywhere(): got = lax.all_gather(block, ('dp', 'expert'), axis=0, tiled=True)]
    unnamed x1 -> x0, blocking collectives: 32.6 us -> none
    all_gather x1 -> x0, blocking collectives: 23.6 us -> none  [everywhere(): got = lax.all_gather(block, ('dp', 'expert'), axis=0, tiled=True)]
    unnamed x7 -> x2, waiting for transfers between devices: 0.76 us -> 19.6 us
    all_to_all x0 -> x1, blocking collectives: none -> 17.3 us  [scatter(): got = lax.all_to_all(cut, 'expert', split_axis=0, concat_axis=0, tiled=True)]
    all_to_all x0 -> x2, starting transfers between devices: none -> 6.77 us  [scatter(): got = lax.all_to_all(cut, 'expert', split_axis=0, concat_axis=0, tiled=True)]
  transfers between devices with their start and end apart: 6 -> 3, of which waited for: 5 -> 2; matrix products, arithmetic and copies ran while one was open for 20% -> 13% of each run, Pallas kernels for 0% -> 0%
where the time goes in v2:
time: 290 us; the launch traced here: 286 us
  matrix products  122 us (42%)
  Pallas kernels  61.4 us (21%)
  waiting for transfers between devices  24 us (8%)
  local copies, waits for them, and re-layouts  23.9 us (8%)
  blocking collectives  17.3 us (6%)
  other arithmetic  16.5 us (6%)
  between operations  14.7 us (5%)
  starting transfers between devices  6.81 us (2%)
    dot_general x10, matrix products, gathered_body(): jnp.einsum(spec, a, b, preferred_element_type=jnp.float32)  96.8 us
    pallas_call x1, Pallas kernels, spread(): pl.pallas_call(spread_kernel, out_shape=[jax.ShapeDtypeStruct((parts, own...  61.4 us
    unnamed x2, waiting for transfers between devices  19.6 us
    all_to_all x1, blocking collectives, scatter(): got = lax.all_to_all(cut, 'expert', split_axis=0, concat_axis=0, tiled=True)  17.3 us
    dot_general x1, matrix products, gathered_body(): jnp.einsum('jsct,std->jscd', pick, tok_grad, preferred_element_type=jnp.f...  14.2 us
    dot_general x1, matrix products, gathered_body(): jnp.einsum('jsct,std->jscd', pick, tok_in, preferred_element_type=jnp.flo...  9.7 us
    convert_element_type x1, local copies, waits for them, and re-layouts, gathered_body(): rows_grad = (slot_weight[..., None] * raw_grad).astype(jnp.bfloat16)  9.21 us
    convert_element_type x1, local copies, waits for them, and re-layouts, gathered_body(): rows_in = jnp.einsum('jsct,std->jscd', pick, tok_in, preferred_element_ty...  9.13 us
  transfers between devices with their start and end apart: 3, of which 2 were waited for; matrix products, arithmetic and copies ran while one was open for 13% of the time, Pallas kernels for 0%

profile of v2, /device:TPU:0, one launch (start us, length us, event | category | flops | bytes accessed | tf_op | source)
XLA Modules:
  0.0 286.4 jit_solution(18258548483610333282)
XLA Ops:
  11.7 61.4 %shard_map.152 = (bf16[4,4,128,1152]{3,2,1,0:T(8,128)(2,1)}, bf16[4,4,128,1024]{3,2,1,0:T(8,128)(2,1)}) custom-call(bf16[128,1152]{1,0:T(8,128)(2,1)} %fusion.45.a_in, bf16[128,1024]{1,0:T(8,128)(2,1)} %b_in.1), custom_call_target="tpu_custom_call" | custom-call | tf_op jit(solution)/shard_map/pallas_call | solution.py:249
  76.1 9.7 %convert_bitcast_fusion = bf16[8,4,144,1024]{3,2,0,1:T(8,128)(2,1)} fusion(s32[8,4,512]{2,0,1:T(8,128)S(1)} %fusion.29, bf16[4,512,1152]{2,1,0:T(8,128)(2,1)} %bitcast.100), kind=kOutput, calls=%fused_computation.8 | convolution fusion | flops 4838916096 | bytes 13697024 | tf_op jit(solution)/shard_map/jsct,std->jscd/dot_general | solution.py:327
  85.8 2.6 iota_compare_fusion
  88.8 1.2 select_reduce_fusion
  90.0 14.2 %fusion = (bf16[8,4,144,1024]{3,2,0,1:T(8,128)(2,1)}, f32[4,1024,8,144]{1,3,2,0:T(8,128)}) fusion(f32[8,4,144]{2,0,1:T(8,128)S(1)} %select_reduce_fusion, bf16[4,512,1024,1]{2,1,3,0:T(8,128)(2,1)} %bitcast.95, s32[8,4,512]{2,0,1:T(8,128)S(1)} %fusion.29), kind=kOutput, calls=%fused_computation.1 | convolution fusion | flops 4843634688 | bytes 32589824 | tf_op jit(solution)/shard_map/jsct,std->jscd/dot_general | solution.py:330
  104.2 9.2 %copy.42 = bf16[8,4,144,1024]{3,2,1,0:T(8,128)(2,1)} copy(bf16[8,4,144,1024]{3,2,0,1:T(8,128)(2,1)} %get-tuple-element.65) | data formatting | bytes 18874368 | tf_op jit(solution)/shard_map/convert_element_type | solution.py:331
  113.4 9.1 %copy.41 = bf16[8,4,144,1024]{3,2,1,0:T(8,128)(2,1)} copy(bf16[8,4,144,1024]{3,2,0,1:T(8,128)(2,1)} %convert_bitcast_fusion) | data formatting | bytes 18874368 | tf_op jit(solution)/shard_map/convert_element_type | solution.py:329
  122.5 12.5 %fusion.63 = f32[8,576,512]{2,1,0:T(8,128)} fusion(bf16[8,576,1024]{2,1,0:T(8,128)(2,1)} %bitcast.90, bf16[8,1024,512]{2,1,0:T(8,128)(2,1)} %param.14), kind=kOutput, calls=%fused_computation.108 | convolution fusion | flops 4831838208 | bytes 27262976 | tf_op jit(solution)/shard_map/jrd,jdf->jrf/dot_general | solution.py:335
  135.0 10.7 %fusion.64 = f32[8,576,512]{2,1,0:T(8,128)} fusion(bf16[8,576,1024]{2,1,0:T(8,128)(2,1)S(1)} %bitcast.93, bf16[8,1024,512]{2,1,0:T(8,128)(2,1)} %param.15), kind=kOutput, calls=%fused_computation.109 | convolution fusion | flops 4831838208 | bytes 27262976 | tf_op jit(solution)/shard_map/jrd,jdf->jrf/dot_general | solution.py:335
  145.7 22.4 %multiply_convert_fusion = (bf16[8,576,512]{2,1,0:T(8,128)(2,1)}, bf16[8,576,512]{2,1,0:T(8,128)(2,1)}, bf16[8,576,512]{2,1,0:T(8,128)(2,1)}) fusion(f32[8,576,512]{2,1,0:T(8,128)} %fusion.63, f32[8,576,512]{2,1,0:T(8,128)} %fusion.64, bf16[8,576,1024]{2,1,0:T(8,128)(2,1)} %bitcast.88, bf16[8,512,1024]{2,1,0:T(8,128)(2,1)} %param.16), kind=kOutput, calls=%fused_computation.2 | convolution fusion | flops 4867227648 | bytes 50855936 | tf_op jit(solution)/shard_map/jrd,jfd->jrf/dot_general | solution.py:335
  168.2 8.8 %fusion.23 = f32[8,144,1024]{2,1,0:T(8,128)} fusion(bf16[8,1024,512]{2,1,0:T(8,128)(2,1)} %param.14, bf16[8,576,512]{2,1,0:T(8,128)(2,1)} %get-tuple-element.55, s32[]{:T(128)S(6)} %select_n.44), kind=kOutput, calls=%fused_computation.40 | convolution fusion | flops 1207959552 | bytes 14286852 | tf_op jit(solution)/shard_map/jcf,jdf->jcd/dot_general | solution.py:335
  177.0 9.6 %bitcast_convert_fusion = bf16[512,1024]{1,0:T(8,128)(2,1)S(1)} fusion(f32[8,144,1024]{2,1,0:T(8,128)} %fusion.23, pred[8,4,144,512]{3,2,0,1:T(8,128)(4,1)} %iota_compare_fusion, s32[]{:T(128)S(6)} %select_n.42, bf16[8,1024,512]{2,1,0:T(8,128)(2,1)} %param.15, bf16[8,576,512]{2,1,0:T(8,128)(2,1)} %get-tuple-element.54, s32[]{:T(128)S(6)} %select_n.44), kind=kOutput, calls=%fused_computation.26 | convolution fusion | flops 2418802688 | bytes 15925256 | tf_op jit(solution)/shard_map/jct,jcd->td/dot_general | solution.py:335
  186.5 17.3 %all_to_all.15 = bf16[4,128,1024]{2,1,0:T(8,128)(2,1)S(1)} all-to-all(bf16[4,128,1024]{2,1,0:T(8,128)(2,1)S(1)} %bitcast.96), channel_id=1, replica_groups=mesh['groups'=2,'expert'=4,'dp'=4] {'expert'}, dimensions={0} | all-to-all | bytes 2097152 | tf_op jit(solution)/shard_map/all_to_all | solution.py:363
  205.5 2.5 copy.47
  208.0 6.7 %fusion.4 = (f32[8,144]{1,0:T(8,128)S(1)}, bf16[8,144,1024]{2,1,0:T(8,128)(2,1)S(1)}) fusion(f32[4,1024,8,144]{1,3,2,0:T(8,128)} %get-tuple-element.66, s32[]{:T(128)S(6)} %select_n.42, bf16[8,512,1024]{2,1,0:T(8,128)(2,1)} %param.16, bf16[8,576,512]{2,1,0:T(8,128)(2,1)} %get-tuple-element.56, s32[]{:T(128)S(6)} %select_n.44), kind=kOutput, calls=%fused_computation.13 | convolution fusion | flops 1212676992 | bytes 16650760 | tf_op jit(solution)/shard_map/jcf,jfd->jcd/dot_general | solution.py:335
  214.8 1.5 select_reduce_fusion.1
  217.1 3.3 %all-to-all-start.2 = ((f32[4,128,8]{1,2,0:T(8,128)}), f32[4,128,8]{1,2,0:T(8,128)S(1)}, u32[]{:S(2)}, u32[]{:S(2)}) async-start(f32[4,128,8]{1,2,0:T(8,128)} %bitcast.29), calls=%async_computation.2 | async-start | bytes 32768 | tf_op jit(solution)/shard_map/all_to_all | solution.py:363
  220.4 3.6 %bitcast_convert_fusion.1 = bf16[512,1024]{1,0:T(8,128)(2,1)} fusion(bf16[8,144,1024]{2,1,0:T(8,128)(2,1)S(1)} %get-tuple-element.68, pred[8,4,144,512]{3,2,0,1:T(8,128)(4,1)} %iota_compare_fusion, s32[]{:T(128)S(6)} %select_n.42, bf16[8,512]{1,0:T(8,128)(2,1)S(1)} %fusion.50), kind=kOutput, calls=%fused_computation.27 | convolution fusion | flops 1209663488 | bytes 4005892 | tf_op jit(solution)/shard_map/jct,jcd->td/dot_general | solution.py:335
  224.0 7.1 %convolution_multiply_fusion = f32[8,256,512]{2,1,0:T(8,128)} fusion(bf16[8,576,512]{2,1,0:T(8,128)(2,1)} %get-tuple-element.54, bf16[8,576,1024]{2,1,0:T(8,128)(2,1)} %bitcast.91, s32[]{:T(128)S(6)} %select_n.48), kind=kOutput, calls=%fused_computation.23 | convolution fusion | flops 1209008128 | bytes 11272196 | tf_op jit(solution)/shard_map/jrd,jrf->jdf/dot_general | solution.py:335
  231.1 3.5 %all-to-all-start = ((bf16[4,128,1024]{2,1,0:T(8,128)(2,1)}), bf16[4,128,1024]{2,1,0:T(8,128)(2,1)S(1)}, u32[]{:S(2)}, u32[]{:S(2)}) async-start(bf16[4,128,1024]{2,1,0:T(8,128)(2,1)} %bitcast.15), calls=%async_computation | async-start | bytes 2097152 | tf_op jit(solution)/shard_map/all_to_all | solution.py:363
  234.6 7.2 %convolution_multiply_fusion.1 = f32[8,256,512]{2,1,0:T(8,128)} fusion(bf16[8,576,512]{2,1,0:T(8,128)(2,1)} %get-tuple-element.55, bf16[8,576,1024]{2,1,0:T(8,128)(2,1)} %bitcast.92, s32[]{:T(128)S(6)} %select_n.48), kind=kOutput, calls=%fused_computation.24 | convolution fusion | flops 1209008128 | bytes 11272196 | tf_op jit(solution)/shard_map/jrd,jrf->jdf/dot_general | solution.py:335
  241.8 8.1 %convolution_multiply_fusion.2 = f32[8,128,1024]{2,1,0:T(8,128)} fusion(bf16[8,576,1024]{2,1,0:T(8,128)(2,1)} %bitcast.89, bf16[8,576,512]{2,1,0:T(8,128)(2,1)} %get-tuple-element.56, s32[]{:T(128)S(6)} %select_n.49), kind=kOutput, calls=%fused_computation.25 | convolution fusion | flops 1209008128 | bytes 14811140 | tf_op jit(solution)/shard_map/jrf,jrd->jfd/dot_general | solution.py:335
  250.5 4.5 %all-to-all-done = bf16[4,128,1024]{2,1,0:T(8,128)(2,1)S(1)} async-done(((bf16[4,128,1024]{2,1,0:T(8,128)(2,1)}), bf16[4,128,1024]{2,1,0:T(8,128)(2,1)S(1)}, u32[]{:S(2)}, u32[]{:S(2)}) %all-to-all-start) | async-done | bytes 1048608 | tf_op jit(solution)/shard_map/all_to_all | solution.py:363
  256.9 19.5 %reduce-scatter.4.cloned.1.call-done = bf16[64,1152]{1,0:T(8,128)(2,1)} async-done(((bf16[1024,1152]{1,0:T(8,128)(2,1)}), bf16[64,1152]{1,0:T(8,128)(2,1)}) %reduce-scatter.4.cloned.1.call-update) | async-done | bytes 147472
  (50 shorter events, 15.3 us)
Async XLA Ops:
  7.2 197.2 %copy-start = (bf16[128,1024]{1,0:T(8,128)(2,1)S(1)}, bf16[128,1024]{1,0:T(8,128)(2,1)}, u32[]{:S(2)}) copy-start(bf16[128,1024]{1,0:T(8,128)(2,1)} %param.10) | copy-start | bytes 786436
  7.2 269.2 %reduce-scatter.4.cloned.1.call-start = ((), (), s32[]{:S(2)}) async-start(), calls=%async_computation.4 | async-start | bytes 2506752
  122.5 12.5 %copy-start.1 = (bf16[8,4,144,1024]{3,2,1,0:T(8,128)(2,1)S(1)}, bf16[8,4,144,1024]{3,2,1,0:T(8,128)(2,1)}, u32[]{:S(2)}) copy-start(bf16[8,4,144,1024]{3,2,1,0:T(8,128)(2,1)} %copy.41) | copy-start | bytes 28311556
  177.0 27.1 %copy-start.2 = (bf16[128,1024]{1,0:T(8,128)(2,1)S(1)}, bf16[128,1024]{1,0:T(8,128)(2,1)}, u32[]{:S(2)}) copy-start(bf16[128,1024]{1,0:T(8,128)(2,1)} %param.9) | copy-start | bytes 786436
  177.0 27.1 %copy-start.4 = (f32[1024]{0:T(1024)S(1)}, f32[1024]{0:T(1024)}, u32[]{:S(2)}) copy-start(f32[1024]{0:T(1024)} %param.11) | copy-start | bytes 12292
  177.0 27.4 %copy-start.3 = (bf16[128,1024]{1,0:T(8,128)(2,1)S(1)}, bf16[128,1024]{1,0:T(8,128)(2,1)}, u32[]{:S(2)}) copy-start(bf16[128,1024]{1,0:T(8,128)(2,1)} %b_in.1) | copy-start | bytes 786436
  217.1 14.0 %all-to-all-start.2 = ((f32[4,128,8]{1,2,0:T(8,128)}), f32[4,128,8]{1,2,0:T(8,128)S(1)}, u32[]{:S(2)}, u32[]{:S(2)}) async-start(f32[4,128,8]{1,2,0:T(8,128)} %bitcast.29), calls=%async_computation.2 | async-start | bytes 32768 | tf_op jit(solution)/shard_map/all_to_all | solution.py:363
  231.1 23.9 %all-to-all-start = ((bf16[4,128,1024]{2,1,0:T(8,128)(2,1)}), bf16[4,128,1024]{2,1,0:T(8,128)(2,1)S(1)}, u32[]{:S(2)}, u32[]{:S(2)}) async-start(bf16[4,128,1024]{2,1,0:T(8,128)(2,1)} %bitcast.15), calls=%async_computation | async-start | bytes 2097152 | tf_op jit(solution)/shard_map/all_to_all | solution.py:363
Sparse Core Ops, SparseCore 0:
  208.1 68.2 reduce-scatter.3

commit v3 on v2

--- a/solution.py
+++ b/solution.py
@@ -1,3 +1,4 @@
+import functools
 import math
 
 import jax
@@ -270,6 +271,82 @@
     return [term.astype(jnp.bfloat16) for term in (high, middle, low)]
 
 
+def expert_kernel(
+    grad_scale, in_ref, raw_ref, weight_ref, gate_ref, up_ref, down_ref,
+    gate_grad, up_grad, down_grad, result, input_delta, act, gate_delta, up_delta,
+):
+    parts, _, super_rows, features = in_ref.shape
+    part = lax.axis_index("dp")
+    rows = parts * super_rows
+    cols, units = gate_grad.shape[1], down_grad.shape[1]
+
+    def dot(a, b, a_dim, b_dim):
+        return lax.dot_general(
+            a, b, (((a_dim,), (b_dim,)), ((), ())), preferred_element_type=jnp.float32
+        )
+
+    rows_in = in_ref[...].reshape(rows, features)
+    raw = raw_ref[...].reshape(rows, features).astype(jnp.float32)
+    rows_grad = (weight_ref[0] * raw).astype(jnp.bfloat16)
+    gate_pre = dot(rows_in, gate_ref[0], 1, 0)
+    up_pre = dot(rows_in, up_ref[0], 1, 0)
+    inner = dot(rows_grad, down_ref[0], 1, 1)
+    logistic = jax.nn.sigmoid(gate_pre)
+    silu = gate_pre * logistic
+    act[...] = (silu * up_pre).astype(jnp.bfloat16)
+    slope = logistic * (1.0 + gate_pre * (1.0 - logistic))
+    gate_delta[...] = (inner * up_pre * slope).astype(jnp.bfloat16)
+    up_delta[...] = (inner * silu).astype(jnp.bfloat16)
+    cut_in = in_ref[:, 0, :, pl.ds(pl.multiple_of(part * cols, cols), cols)].reshape(rows, cols)
+    cut_act = act[:, pl.ds(pl.multiple_of(part * units, units), units)]
+    gate_grad[0] = dot(cut_in, gate_delta[...], 0, 0) * grad_scale
+    up_grad[0] = dot(cut_in, up_delta[...], 0, 0) * grad_scale
+    down_grad[0] = dot(cut_act, rows_grad, 0, 0) * grad_scale
+    own = pl.ds(pl.multiple_of(part * super_rows, super_rows), super_rows)
+    result[0] = dot(act[own, :], down_ref[0], 1, 0).astype(jnp.bfloat16)
+    input_delta[0] = (
+        dot(gate_delta[own, :], gate_ref[0], 1, 1) + dot(up_delta[own, :], up_ref[0], 1, 1)
+    ).astype(jnp.bfloat16)
+
+
+def run_experts(rows_in, raw_grad, slot_weight, w_gate, w_up, w_down, grad_scale):
+    parts, local_experts, super_rows, features = rows_in.shape
+    hidden_units = w_gate.shape[2]
+    rows = parts * super_rows
+    block = lambda *shape: pl.BlockSpec((1, *shape), lambda j: (j, 0, 0))
+    slots = pl.BlockSpec((parts, 1, super_rows, features), lambda j: (0, j, 0, 0))
+    whole = lambda kind, *shape: jax.ShapeDtypeStruct((local_experts, *shape), kind)
+    cols, units = features // parts, hidden_units // parts
+    return pl.pallas_call(
+        functools.partial(expert_kernel, grad_scale),
+        grid=(local_experts,),
+        in_specs=[
+            slots,
+            slots,
+            block(rows, 1),
+            block(features, hidden_units),
+            block(features, hidden_units),
+            block(hidden_units, features),
+        ],
+        out_specs=[
+            block(cols, hidden_units),
+            block(cols, hidden_units),
+            block(units, features),
+            block(super_rows, features),
+            block(super_rows, features),
+        ],
+        out_shape=[
+            whole(jnp.float32, cols, hidden_units),
+            whole(jnp.float32, cols, hidden_units),
+            whole(jnp.float32, units, features),
+            whole(jnp.bfloat16, super_rows, features),
+            whole(jnp.bfloat16, super_rows, features),
+        ],
+        scratch_shapes=[pltpu.VMEM((rows, hidden_units), jnp.bfloat16)] * 3,
+        compiler_params=pltpu.CompilerParams(vmem_limit_bytes=48 * 2**20),
+    )(rows_in, raw_grad, slot_weight, w_gate, w_up, w_down)
+
+
 def token_rows(ids, local_experts, capacity, first_expert):
     blocks, owners, tok_rows, _ = ids.shape
     named = first_expert + jnp.arange(local_experts, dtype=jnp.int32)
@@ -287,7 +364,7 @@
 def gathered_body(hidden_in, context, norm_gain, route_ids, route_weights, w_gate, w_up, w_down, out_grad):
     tok_rows, feature_count = hidden_in.shape
     top_count = route_ids.shape[1]
-    local_experts, _, hidden_units = w_gate.shape
+    local_experts = w_gate.shape[0]
     owners, parts = lax.axis_size("expert"), lax.axis_size("dp")
     expert_at, part_at = lax.axis_index("expert"), lax.axis_index("dp")
     capacity = tok_rows * top_count * 9 // (8 * local_experts * owners)
@@ -319,38 +396,25 @@
     match = ids[..., None] == named
     tok_weight = jnp.sum(jnp.where(match, weights[..., None], 0.0), axis=2)
     slots = jnp.arange(super_rows, dtype=jnp.int32)
-    pick_mask = row.transpose(2, 0, 1)[:, :, None, :] == slots[:, None]
+    pick_mask = row.transpose(0, 2, 1)[:, :, None, :] == slots[:, None]
     pick = pick_mask.astype(jnp.bfloat16)
     slot_weight = jnp.sum(
-        jnp.where(pick_mask, tok_weight.transpose(2, 0, 1)[:, :, None, :], 0.0), axis=-1
-    )
-    rows_in = jnp.einsum(
-        "jsct,std->jscd", pick, tok_in, preferred_element_type=jnp.float32
-    ).astype(jnp.bfloat16)
-    raw_grad = jnp.einsum("jsct,std->jscd", pick, tok_grad, preferred_element_type=jnp.float32)
-    rows_grad = (slot_weight[..., None] * raw_grad).astype(jnp.bfloat16)
-    flat = (local_experts, parts * super_rows)
-    rows_in = rows_in.reshape(*flat, feature_count)
-    rows_grad = rows_grad.reshape(*flat, feature_count)
+        jnp.where(pick_mask, tok_weight.transpose(0, 2, 1)[:, :, None, :], 0.0), axis=-1
+    )
+    slot_weight = slot_weight.transpose(1, 0, 2).reshape(local_experts, parts * super_rows, 1)
     dot = lambda spec, a, b: jnp.einsum(spec, a, b, preferred_element_type=jnp.float32)
-    gate_pre = dot("jrd,jdf->jrf", rows_in, w_gate)
-    up_pre = dot("jrd,jdf->jrf", rows_in, w_up)
-    hidden_act = (jax.nn.silu(gate_pre) * up_pre).astype(jnp.bfloat16)
-    inner_grad = dot("jrd,jfd->jrf", rows_grad, w_down)
-    gate_delta = (inner_grad * up_pre * silu_slope(gate_pre)).astype(jnp.bfloat16)
-    up_delta = (inner_grad * jax.nn.silu(gate_pre)).astype(jnp.bfloat16)
-
-    def own(rows):
-        return lax.dynamic_slice_in_dim(rows, part_at * super_rows, super_rows, axis=1)
-
-    own_pick = lax.dynamic_index_in_dim(pick, part_at, axis=1, keepdims=False)
+    flat_pick = pick.reshape(parts, local_experts * super_rows, super_toks)
+    slot_shape = (parts, local_experts, super_rows, feature_count)
+    rows_in = dot("srt,std->srd", flat_pick, tok_in).astype(jnp.bfloat16).reshape(slot_shape)
+    raw_grad = dot("srt,std->srd", flat_pick, tok_grad).astype(jnp.bfloat16).reshape(slot_shape)
+    gate_grad, up_grad, down_grad, result, input_delta = run_experts(
+        rows_in, raw_grad, slot_weight, w_gate, w_up, w_down, grad_scale
+    )
+    own_pick = lax.dynamic_index_in_dim(pick, part_at, axis=0, keepdims=False)
     own_weight = lax.dynamic_index_in_dim(tok_weight, part_at, axis=0, keepdims=False)
     own_match = lax.dynamic_index_in_dim(match, part_at, axis=0, keepdims=False)
-    own_raw = lax.dynamic_index_in_dim(raw_grad, part_at, axis=1, keepdims=False)
-    result = dot("jcf,jfd->jcd", own(hidden_act), w_down).astype(jnp.bfloat16)
-    input_delta = (
-        dot("jcf,jdf->jcd", own(gate_delta), w_gate) + dot("jcf,jdf->jcd", own(up_delta), w_up)
-    ).astype(jnp.bfloat16)
+    own_raw = lax.dynamic_index_in_dim(raw_grad, part_at, axis=0, keepdims=False)
+    own_raw = own_raw.astype(jnp.float32)
     weighted = own_pick * own_weight.T.astype(jnp.bfloat16)[:, None, :]
     moe_term = dot("jct,jcd->td", weighted, result).astype(jnp.bfloat16)
     delta_term = dot("jct,jcd->td", own_pick, input_delta).astype(jnp.bfloat16)
@@ -366,13 +430,6 @@
     norm_delta = scatter(delta_term)
     moe_out = scatter(moe_term).astype(jnp.bfloat16)
     route_grad = scatter(route_term)
-
-    cols, units = feature_count // parts, hidden_units // parts
-    cut_in = lax.dynamic_slice_in_dim(rows_in, part_at * cols, cols, axis=2)
-    cut_act = lax.dynamic_slice_in_dim(hidden_act, part_at * units, units, axis=2)
-    gate_grad = dot("jrd,jrf->jdf", cut_in, gate_delta) * grad_scale
-    up_grad = dot("jrd,jrf->jdf", cut_in, up_delta) * grad_scale
-    down_grad = dot("jrf,jrd->jfd", cut_act, rows_grad) * grad_scale
 
     scaled_delta = norm_delta * norm_gain
     branch = inv_rms * (

time: 290 us -> 235 us (0.81); the launches traced: 286 us -> 235 us
  matrix products: 122 us -> 24.7 us
  Pallas kernels: 61.4 us -> 94.9 us
  waiting for transfers between devices: 24 us -> 44.9 us
  local copies, waits for them, and re-layouts: 23.9 us -> 10.1 us
  other arithmetic: 16.5 us -> 21.7 us
    dot_general x10 -> x4, matrix products: 96.8 us -> 23.6 us  [gathered_body(): jnp.einsum(spec, a, b, preferred_element_type=jnp.float32)]
    pallas_call x0 -> x1, Pallas kernels: none -> 33.5 us  [run_experts(): pl.pallas_call(functools.partial(expert_kernel, grad_scale), grid=(local_...]
    dot_general x2 -> x0, matrix products: 23.9 us -> none  [the longest x1 14.2 us: gathered_body(): jnp.einsum('jsct,std->jscd', pick, tok_grad, preferred_element_type=jnp.f...]
    convert_element_type x2 -> x0, local copies, waits for them, and re-layouts: 18.3 us -> none  [the longest x1 9.21 us: gathered_body(): rows_grad = (slot_weight[..., None] * raw_grad).astype(jnp.bfloat16)]
    unnamed x2, waiting for transfers between devices: 19.6 us -> 31 us
    all_to_all x2, waiting for transfers between devices: 4.49 us -> 14 us  [scatter(): got = lax.all_to_all(cut, 'expert', split_axis=0, concat_axis=0, tiled=True)]
  transfers between devices with their start and end apart: 3 -> 3, of which waited for: 2 -> 3; matrix products, arithmetic and copies ran while one was open for 13% -> 5% of each run, Pallas kernels for 0% -> 0%
where the time goes in v3:
time: 235 us
  Pallas kernels  94.9 us (40%)
  waiting for transfers between devices  44.9 us (19%)
  matrix products  24.7 us (11%)
  other arithmetic  21.7 us (9%)
  blocking collectives  17.2 us (7%)
  between operations  14.3 us (6%)
  local copies, waits for them, and re-layouts  10.1 us (4%)
  starting transfers between devices  6.81 us (3%)
    pallas_call x1, Pallas kernels, spread(): pl.pallas_call(spread_kernel, out_shape=[jax.ShapeDtypeStruct((parts, own...  61.4 us
    pallas_call x1, Pallas kernels, run_experts(): pl.pallas_call(functools.partial(expert_kernel, grad_scale), grid=(local_...  33.5 us
    unnamed x2, waiting for transfers between devices  31 us
    dot_general x4, matrix products, gathered_body(): jnp.einsum(spec, a, b, preferred_element_type=jnp.float32)  23.6 us
    all_to_all x1, blocking collectives, scatter(): got = lax.all_to_all(cut, 'expert', split_axis=0, concat_axis=0, tiled=True)  17.2 us
    all_to_all x2, waiting for transfers between devices, scatter(): got = lax.all_to_all(cut, 'expert', split_axis=0, concat_axis=0, tiled=True)  14 us
    all_to_all x2, starting transfers between devices, scatter(): got = lax.all_to_all(cut, 'expert', split_axis=0, concat_axis=0, tiled=True)  6.78 us
    unnamed x13, local copies, waits for them, and re-layouts  6.36 us
  transfers between devices with their start and end apart: 3, of which 3 were waited for; matrix products, arithmetic and copies ran while one was open for 5% of the time, Pallas kernels for 0%

profile of v3, /device:TPU:0, one launch (start us, length us, event | category | flops | bytes accessed | tf_op | source)
XLA Modules:
  0.0 234.6 jit_solution(15280384947250106866)
XLA Ops:
  8.8 1.1 fusion.26
  9.9 1.1 fusion.21
  11.7 61.4 %shard_map.152 = (bf16[4,4,128,1152]{3,2,1,0:T(8,128)(2,1)}, bf16[4,4,128,1024]{3,2,1,0:T(8,128)(2,1)}) custom-call(bf16[128,1152]{1,0:T(8,128)(2,1)} %fusion.30.a_in, bf16[128,1024]{1,0:T(8,128)(2,1)} %b_in.1), custom_call_target="tpu_custom_call" | custom-call | tf_op jit(solution)/shard_map/pallas_call | solution.py:250
  73.1 1.1 slice_convert_fusion.1
  76.4 2.6 %iota_compare_fusion = pred[4,8,144,512]{3,2,1,0:T(8,128)(4,1)} fusion(s32[4,8,512]{2,1,0:T(8,128)S(1)} %fusion.14), kind=kLoop, calls=%fused_computation.4 | loop fusion | flops 2359296 | bytes 2424832 | tf_op jit(solution)/shard_map/eq | solution.py:399
  79.1 1.2 select_reduce_fusion
  80.3 2.5 %reshape.134.weight_ref = f32[8,576,1]{2,1,0:T(8,128)} reshape(f32[8,4,144]{2,1,0:T(4,128)S(1)} %copy.40) | data formatting | bytes 36864 | tf_op jit(solution)/shard_map/reshape | solution.py:404
  83.0 1.4 bitcast_compare_fusion
  84.4 9.9 %convolution_convert_fusion.1 = bf16[4,1152,1024]{2,1,0:T(8,128)(2,1)} fusion(pred[4,1152,512]{2,1,0:T(32,128)(4,1)S(1)} %bitcast_compare_fusion, bf16[4,512,1152]{2,1,0:T(8,128)(2,1)} %bitcast.74), kind=kOutput, calls=%fused_computation.1 | convolution fusion | flops 4836556800 | bytes 15990784 | tf_op jit(solution)/shard_map/srt,std->srd/dot_general | solution.py:405
  94.3 7.4 %convolution_convert_fusion = bf16[4,1152,1024]{2,1,0:T(8,128)(2,1)} fusion(pred[4,1152,512]{2,1,0:T(32,128)(4,1)S(1)} %bitcast_compare_fusion, bf16[4,512,1024]{2,1,0:T(8,128)(2,1)S(1)} %bitcast.76), kind=kOutput, calls=%fused_computation | convolution fusion | flops 4836556800 | bytes 15990784 | tf_op jit(solution)/shard_map/srt,std->srd/dot_general | solution.py:405
  101.8 33.5 %shard_map.153 = (f32[8,256,512]{2,1,0:T(8,128)}, f32[8,256,512]{2,1,0:T(8,128)}, f32[8,128,1024]{2,1,0:T(8,128)}, bf16[8,144,1024]{2,1,0:T(8,128)(2,1)S(1)}, bf16[8,144,1024]{2,1,0:T(8,128)(2,1)S(1)}) custom-call(bf16[4,8,144,1024]{3,2,1,0:T(8,128)(2,1)} %bitcast.67, bf16[4,8,144,1024]{3,2,1,0:T(8,128)(2,1)} %bitcast.64, f32[8,576,1]{2,1,0:T(8,128)} %reshape.134.weight_ref, ...), custom_call_target="tpu_custom_call" | custom-call | tf_op jit(solution)/shard_map/pallas_call | solution.py:320
  135.3 2.6 %bitcast_convert_fusion = bf16[512,1024]{1,0:T(8,128)(2,1)S(1)} fusion(bf16[8,144,1024]{2,1,0:T(8,128)(2,1)S(1)} %get-tuple-element.18, pred[4,8,144,512]{3,2,1,0:T(8,128)(4,1)} %iota_compare_fusion, s32[]{:T(128)S(6)} %select_n.31), kind=kOutput, calls=%fused_computation.13 | convolution fusion | flops 1208483840 | bytes 3997700 | tf_op jit(solution)/shard_map/jct,jcd->td/dot_general | solution.py:405
  137.9 17.2 %all_to_all.15 = bf16[4,128,1024]{2,1,0:T(8,128)(2,1)S(1)} all-to-all(bf16[4,128,1024]{2,1,0:T(8,128)(2,1)S(1)} %bitcast.69), channel_id=1, replica_groups=mesh['groups'=2,'expert'=4,'dp'=4] {'expert'}, dimensions={0} | all-to-all | bytes 2097152 | tf_op jit(solution)/shard_map/all_to_all | solution.py:427
  156.6 1.7 pad_maximum_fusion
  158.3 4.3 %copy.44 = bf16[1024,1152]{1,0:T(8,128)(2,1)} copy(bf16[1024,1152]{0,1:T(8,128)(2,1)} %pad_maximum_fusion) | data formatting | bytes 4718592
  162.6 2.4 %fusion = f32[8,144]{1,0:T(8,128)S(1)} fusion(bf16[8,144,1024]{2,1,0:T(8,128)(2,1)S(1)} %get-tuple-element.17, bf16[4,8,144,1024]{3,2,1,0:T(8,128)(2,1)} %bitcast.65, s32[]{:T(128)S(6)} %select_n.31), kind=kLoop, calls=%fused_computation.6 | loop fusion | flops 4717440 | bytes 4723204 | tf_op jit(solution)/shard_map/reduce_sum | solution.py:421
  165.0 1.5 select_reduce_fusion.1
  167.3 3.3 %all-to-all-start.2 = ((f32[4,128,8]{1,2,0:T(8,128)}), f32[4,128,8]{1,2,0:T(8,128)S(1)}, u32[]{:S(2)}, u32[]{:S(2)}) async-start(f32[4,128,8]{1,2,0:T(8,128)} %bitcast.24), calls=%async_computation.2 | async-start | bytes 32768 | tf_op jit(solution)/shard_map/all_to_all | solution.py:427
  170.6 3.6 %bitcast_convert_fusion.1 = bf16[512,1024]{1,0:T(8,128)(2,1)} fusion(bf16[8,144,1024]{2,1,0:T(8,128)(2,1)S(1)} %get-tuple-element.17, pred[4,8,144,512]{3,2,1,0:T(8,128)(4,1)} %iota_compare_fusion, s32[]{:T(128)S(6)} %select_n.31, bf16[8,512]{1,0:T(8,128)(2,1)S(1)} %fusion.35), kind=kOutput, calls=%fused_computation.14 | convolution fusion | flops 1209663488 | bytes 4005892 | tf_op jit(solution)/shard_map/jct,jcd->td/dot_general | solution.py:405
  174.4 3.5 %all-to-all-start = ((bf16[4,128,1024]{2,1,0:T(8,128)(2,1)}), bf16[4,128,1024]{2,1,0:T(8,128)(2,1)S(1)}, u32[]{:S(2)}, u32[]{:S(2)}) async-start(bf16[4,128,1024]{2,1,0:T(8,128)(2,1)} %bitcast.68), calls=%async_computation | async-start | bytes 2097152 | tf_op jit(solution)/shard_map/all_to_all | solution.py:427
  178.5 13.8 %all-to-all-done = bf16[4,128,1024]{2,1,0:T(8,128)(2,1)S(1)} async-done(((bf16[4,128,1024]{2,1,0:T(8,128)(2,1)}), bf16[4,128,1024]{2,1,0:T(8,128)(2,1)S(1)}, u32[]{:S(2)}, u32[]{:S(2)}) %all-to-all-start) | async-done | bytes 1048608 | tf_op jit(solution)/shard_map/all_to_all | solution.py:427
  192.4 0.9 reduce_sum.114
  194.2 30.9 %reduce-scatter.4.cloned.1.call-done = bf16[64,1152]{1,0:T(8,128)(2,1)} async-done(((bf16[1024,1152]{1,0:T(8,128)(2,1)}), bf16[64,1152]{1,0:T(8,128)(2,1)}) %reduce-scatter.4.cloned.1.call-update) | async-done | bytes 147472
  225.1 1.1 copy.45
  (47 shorter events, 10.1 us)
Async XLA Ops:
  7.2 148.5 %copy-start = (bf16[128,1024]{1,0:T(8,128)(2,1)S(1)}, bf16[128,1024]{1,0:T(8,128)(2,1)}, u32[]{:S(2)}) copy-start(bf16[128,1024]{1,0:T(8,128)(2,1)} %param.10) | copy-start | bytes 786436
  7.2 218.0 %reduce-scatter.4.cloned.1.call-start = ((), (), s32[]{:S(2)}) async-start(), calls=%async_computation.4 | async-start | bytes 2506752
  84.4 9.9 %copy-start.4 = (bf16[4,4,128,1024]{3,2,1,0:T(8,128)(2,1)S(1)}, bf16[4,4,128,1024]{3,2,1,0:T(8,128)(2,1)}, u32[]{:S(2)}) copy-start(bf16[4,4,128,1024]{3,2,1,0:T(8,128)(2,1)} %get-tuple-element.16) | copy-start | bytes 12582916
  137.9 17.4 %copy-start.1 = (bf16[128,1024]{1,0:T(8,128)(2,1)S(1)}, bf16[128,1024]{1,0:T(8,128)(2,1)}, u32[]{:S(2)}) copy-start(bf16[128,1024]{1,0:T(8,128)(2,1)} %param.9) | copy-start | bytes 786436
  137.9 17.4 %copy-start.3 = (f32[1024]{0:T(1024)S(1)}, f32[1024]{0:T(1024)}, u32[]{:S(2)}) copy-start(f32[1024]{0:T(1024)} %param.11) | copy-start | bytes 12292
  137.9 17.7 %copy-start.2 = (bf16[128,1024]{1,0:T(8,128)(2,1)S(1)}, bf16[128,1024]{1,0:T(8,128)(2,1)}, u32[]{:S(2)}) copy-start(bf16[128,1024]{1,0:T(8,128)(2,1)} %b_in.1) | copy-start | bytes 786436
  167.3 7.1 %all-to-all-start.2 = ((f32[4,128,8]{1,2,0:T(8,128)}), f32[4,128,8]{1,2,0:T(8,128)S(1)}, u32[]{:S(2)}, u32[]{:S(2)}) async-start(f32[4,128,8]{1,2,0:T(8,128)} %bitcast.24), calls=%async_computation.2 | async-start | bytes 32768 | tf_op jit(solution)/shard_map/all_to_all | solution.py:427
  174.4 18.0 %all-to-all-start = ((bf16[4,128,1024]{2,1,0:T(8,128)(2,1)}), bf16[4,128,1024]{2,1,0:T(8,128)(2,1)S(1)}, u32[]{:S(2)}, u32[]{:S(2)}) async-start(bf16[4,128,1024]{2,1,0:T(8,128)(2,1)} %bitcast.68), calls=%async_computation | async-start | bytes 2097152 | tf_op jit(solution)/shard_map/all_to_all | solution.py:427
Sparse Core Ops, SparseCore 0:
  162.8 62.3 reduce-scatter.3
